TPU v7x, 128 devices: a whole 4x4x4 slice. The times are simulated.
128 devices in a mesh: lon: 32 (over x, y_hi, z), lat: 4 (over y_lo, core).
Axes of the slice: x: 4, y: 4 (y_hi: 2, y_lo: 2; y = y_hi * 2 + y_lo), z: 4, core: 2. Of those that a mesh axis runs over, the one named last changes fastest.
Arguments:
- states: bfloat16 [2, 64, 2048, 192], P(None, 'lat', 'lon'), may hold values from -6 to 6
- grad_out: bfloat16 [64, 2048, 192], P('lat', 'lon'), may hold values from -6 to 6
- land_mask: int32 [64, 2048], P('lat', 'lon'), may hold values 0 or 1
- partner: int32 [2048], replicated, may hold values from 0 to 2047, as said below
- dw_kernel: float32 [7, 7, 192], replicated, may hold values from -0.875 to 0.875
- dw_bias: float32 [192], replicated, may hold values from -3 to 3
- ln_gain: float32 [192], replicated, may hold values from 0.1 to 1.9
- ln_bias: float32 [192], replicated, may hold values from -2 to 2
- w_in: bfloat16 [192, 768], replicated, may hold values from -0.4375 to 0.4375
- b_in: float32 [768], replicated, may hold values from -2 to 2
- w_out: bfloat16 [768, 192], replicated, may hold values from -0.21875 to 0.21875
- b_out: float32 [192], replicated, may hold values from -2 to 2
- layer_scale: float32 [192], replicated, may hold values from 0.3 to 1
Outputs:
- out_a: bfloat16 [64, 2048, 192], P('lat', 'lon')
- grad_states: float32 [64, 2048, 192], P('lat', 'lon')
- grad_kernel: float32 [7, 7, 192], replicated
- grad_win: float32 [192, 768], replicated
- grad_wout: float32 [768, 192], replicated
Inputs may be any that keep to these rules, and one draw needn't show every extreme that they name: partner[j] = (2047 - j + s) mod 2048 for one shift s, the same for all j: a mirror of the columns, so each column appears exactly once.
All inputs are finite; a program needn't handle non-finite values. No bound on the sum of `land_mask` on one device may be relied on, other than what follows from the above.
Results may differ from a plain program's by a relative error of at most 0.0062.
Values may be sent and summed in bfloat16 or wider, within the bound.
A program may use at most 192 MiB of HBM per device.

v0:
```python
import math

import jax
import jax.numpy as jnp
from jax import lax
from jax.sharding import PartitionSpec as P

root_factor = math.sqrt(2.0 / math.pi)
cubic_coef = 0.044715
norm_eps = 1e-06


def extended_2(block, sides, width):
    for axis, dim in sides:
        count = lax.axis_size(axis)
        forward = [(i, i + 1) for i in range(count - 1)]
        forward.append((count - 1, 0))
        backward = [(target, source) for source, target in forward]
        low = lax.ppermute(
            lax.slice_in_dim(block, block.shape[dim] - width, None, axis=dim), axis, forward
        )
        high = lax.ppermute(lax.slice_in_dim(block, 0, width, axis=dim), axis, backward)
        block = jnp.concatenate([low, block, high], axis=dim)
    return block


def gelu_pair(hidden):
    tangent = jnp.tanh(root_factor * (hidden + cubic_coef * hidden * hidden * hidden))
    value = 0.5 * hidden * (1.0 + tangent)
    slope = 0.5 * (1.0 + tangent) + 0.5 * hidden * (1.0 - tangent * tangent) * root_factor * (
        1.0 + 3.0 * cubic_coef * hidden * hidden
    )
    return (value, slope)


def cell_forward(depth_out, ln_gain, ln_bias, w_in, b_in, w_out, b_out):
    centre = jnp.mean(depth_out, axis=-1, keepdims=True)
    centred = depth_out - centre
    inv_std = lax.rsqrt(jnp.mean(centred * centred, axis=-1, keepdims=True) + norm_eps)
    normed = centred * inv_std
    lowered = (normed * ln_gain + ln_bias).astype(jnp.bfloat16)
    hidden = jnp.dot(lowered, w_in, preferred_element_type=jnp.float32) + b_in
    value, slope = gelu_pair(hidden)
    active = value.astype(jnp.bfloat16)
    mixed = jnp.dot(active, w_out, preferred_element_type=jnp.float32) + b_out
    return (mixed, (normed, inv_std, lowered, slope, active))


def cell_backward(grad_mixed, saved, ln_gain, w_in, w_out):
    normed, inv_std, lowered, slope, active = saved
    grad_low = grad_mixed.astype(jnp.bfloat16)
    grad_wout = lax.dot_general(
        active, grad_low, (((0,), (0,)), ((), ())), preferred_element_type=jnp.float32
    )
    grad_act = lax.dot_general(
        grad_low, w_out, (((1,), (1,)), ((), ())), preferred_element_type=jnp.float32
    )
    grad_hid = (grad_act * slope).astype(jnp.bfloat16)
    grad_win = lax.dot_general(
        lowered, grad_hid, (((0,), (0,)), ((), ())), preferred_element_type=jnp.float32
    )
    grad_norm = (
        lax.dot_general(
            grad_hid, w_in, (((1,), (1,)), ((), ())), preferred_element_type=jnp.float32
        )
        * ln_gain
    )
    mean_one = jnp.mean(grad_norm, axis=-1, keepdims=True)
    mean_two = jnp.mean(grad_norm * normed, axis=-1, keepdims=True)
    grad_z = inv_std * (grad_norm - mean_one - normed * mean_two)
    return (grad_z, grad_win, grad_wout)


def depthwise(padded, kernel, rows, cols):
    total = jnp.zeros((rows, cols, padded.shape[2]), jnp.float32)
    for row_off in range(7):
        for col_off in range(7):
            total = total + kernel[row_off, col_off] * padded[
                row_off : row_off + rows, col_off : col_off + cols
            ].astype(jnp.float32)
    return total


def shards(
    states,
    grad_out,
    land_mask,
    partner,
    dw_kernel,
    dw_bias,
    ln_gain,
    ln_bias,
    w_in,
    b_in,
    w_out,
    b_out,
    layer_scale,
):
    rows = states.shape[1]
    cols = states.shape[2]
    chans = states.shape[3]
    lat_count = lax.axis_size("lat")
    lon_count = lax.axis_size("lon")
    band = lax.axis_index("lat")
    column_block = lax.axis_index("lon")
    full_lon = cols * lon_count
    is_top = band == lat_count - 1
    ext_cols = (column_block * cols + jnp.arange(cols + 6, dtype=jnp.int32) - 3) % full_lon
    fold_cols = jnp.take(partner, ext_cols)
    padded = extended_2(states, (("lat", 1), ("lon", 2)), 3)
    top_rows = states[:, rows - 3 :]
    band_rows = lax.all_gather(top_rows, "lon", axis=2, tiled=True)
    north = jnp.take(band_rows[:, ::-1], fold_cols, axis=2)
    south = jnp.where(band == 0, jnp.zeros_like(padded[:, :3]), padded[:, :3])
    north = jnp.where(is_top, north, padded[:, rows + 3 :])
    padded = jnp.concatenate([south, padded[:, 3 : rows + 3], north], axis=1)
    cells = rows * cols
    masks = land_mask.astype(jnp.float32).reshape(cells, 1)
    depth_a = depthwise(padded[0], dw_kernel, rows, cols) + dw_bias
    depth_b = depthwise(padded[1], dw_kernel, rows, cols) + dw_bias
    mixed_a, unused = cell_forward(
        depth_a.reshape(cells, chans), ln_gain, ln_bias, w_in, b_in, w_out, b_out
    )
    out_a = (
        states[0].reshape(cells, chans).astype(jnp.float32) + masks * (layer_scale * mixed_a)
    ).astype(jnp.bfloat16)
    out_a = out_a.reshape(rows, cols, chans)
    mixed_b, saved = cell_forward(
        depth_b.reshape(cells, chans), ln_gain, ln_bias, w_in, b_in, w_out, b_out
    )
    grad_mixed = masks * (layer_scale * grad_out.reshape(cells, chans).astype(jnp.float32))
    grad_flat, grad_win, grad_wout = cell_backward(grad_mixed, saved, ln_gain, w_in, w_out)
    grad_z = grad_flat.reshape(rows, cols, chans)
    kernel_rows = []
    for row_off in range(7):
        kernel_rows.append(
            jnp.stack(
                [
                    jnp.sum(
                        padded[1, row_off : row_off + rows, col_off : col_off + cols].astype(
                            jnp.float32
                        )
                        * grad_z,
                        axis=(0, 1),
                    )
                    for col_off in range(7)
                ]
            )
        )
    grad_kernel = jnp.stack(kernel_rows)
    zero_pad = jnp.pad(grad_z, ((6, 6), (6, 6), (0, 0)))
    grad_pad = jnp.zeros((rows + 6, cols + 6, chans), jnp.float32)
    for row_off in range(7):
        for col_off in range(7):
            grad_pad = (
                grad_pad
                + dw_kernel[row_off, col_off]
                * zero_pad[6 - row_off : 12 - row_off + rows, 6 - col_off : 12 - col_off + cols]
            )
    extended = extended_2(grad_pad.astype(jnp.bfloat16), (("lat", 0), ("lon", 1)), 3).astype(
        grad_pad.dtype
    )
    south_keep = (band > 0).astype(jnp.float32)
    north_keep = (band < lat_count - 1).astype(jnp.float32)
    row_parts = (
        (0, 3, 0, south_keep),
        (6, rows + 6, 0, 1.0),
        (rows + 9, rows + 12, rows - 3, north_keep),
    )
    col_parts = ((0, 3, 0), (6, cols + 6, 0), (cols + 9, cols + 12, cols - 3))
    returned = jnp.zeros((rows, cols, chans), jnp.float32)
    for row_start, row_end, row_dest, weight_keep in row_parts:
        for col_start, col_end, col_dest in col_parts:
            block = extended[row_start:row_end, col_start:col_end] * weight_keep
            returned = returned + jnp.pad(
                block,
                (
                    (row_dest, rows - row_dest - (row_end - row_start)),
                    (col_dest, cols - col_dest - (col_end - col_start)),
                    (0, 0),
                ),
            )
    ghost = grad_pad[rows + 3 :] * is_top.astype(jnp.float32)
    term = jnp.zeros((3, full_lon, chans), jnp.float32).at[:, fold_cols].add(ghost)
    share = lax.psum_scatter(
        term.astype(jnp.bfloat16), "lon", scatter_dimension=1, tiled=True
    ).astype(jnp.float32)
    returned = returned + jnp.pad(share[::-1], ((rows - 3, 0), (0, 0), (0, 0)))
    grad_states = grad_out.astype(jnp.float32) + returned
    totals = lax.psum((grad_kernel, grad_win, grad_wout), ("lon", "lat"))
    scale = 1.0 / math.sqrt(rows * lat_count * cols * lon_count)
    return (out_a, grad_states, totals[0] * scale, totals[1] * scale, totals[2] * scale)


def solution(mesh):
    placed = (
        P(None, "lat", "lon", None),
        P("lat", "lon", None),
        P("lat", "lon"),
        P(),
        P(),
        P(),
        P(),
        P(),
        P(),
        P(),
        P(),
        P(),
        P(),
    )
    return jax.shard_map(
        shards,
        mesh=mesh,
        in_specs=placed,
        out_specs=(P("lat", "lon", None), P("lat", "lon", None), P(), P(), P()),
        check_vma=False,
    )
```

profile of v0, /device:TPU:0, one launch (start us, length us, event | category | flops | bytes accessed | tf_op | source)
XLA Modules:
  0.0 927.3 jit_solution(10499641187745572496)
XLA Ops:
  19.6 7.0 collective-permute-start.3
  44.0 2.8 bitcast_convert_fusion.23
  51.6 2.7 bitcast_convert_fusion.21
  59.3 46.6 %all-gather.2.cloned.1.call-done = bf16[2,3,2048,192]{3,0,1,2:T(2,128)(2,1)} async-done(((bf16[2,3,64,192]{3,0,1,2:T(2,128)(2,1)}), bf16[2,3,2048,192]{3,0,1,2:T(2,128)(2,1)}) %all-gather.2.cloned.1.call-update) | async-done | bytes 4718608 | tf_op jit(solution)/shard_map/all_gather | solution.py:112
  105.9 6.9 copy.579
  112.8 11.0 %rev.6 = bf16[2,3,2048,192]{3,0,2,1:T(2,128)(2,1)} reverse(bf16[2,3,2048,192]{3,0,2,1:T(2,128)(2,1)} %copy.579), dimensions={1} | reverse | bytes 9437184 | tf_op jit(solution)/shard_map/rev | solution.py:113
  123.8 4.6 gather_fusion.1
  131.0 9.2 fusion.188
  152.5 3.0 fusion.185
  165.1 2.8 fusion.157
  307.3 2.7 bitcast_convert_fusion.36
  318.4 7.4 multiply_reduce_fusion.2
  327.5 5.3 multiply_reduce_fusion.38
  333.3 37.4 %fusion.186 = (bf16[22,70,192]{2,1,0:T(8,128)(2,1)S(1)}, f32[22,70,192]{2,1,0:T(8,128)S(1)}) fusion(f32[192]{0:T(256)S(1)} %bitcast.325, f32[192]{0:T(256)S(1)} %bitcast.328, f32[192]{0:T(256)S(1)} %bitcast.334, f32[192]{0:T(256)S(1)} %bitcast.337, f32[192]{0:T(256)S(1)} %bitcast.340, f32[192]{0:T(256)S(1)} %bitcast.343, f32[192]{0:T(256)S(1)} %bitcast.346, ...), kind=kLoop, calls=%fused_computation.453 | loop fusion | flops 28976640 | bytes 2598144 | tf_op jit(solution)/shard_map/convert_element_type | solution.py:160
  373.2 4.1 broadcast_in_dim.27
  377.4 8.8 scatter_fusion
  386.3 6.4 convert_element_type.831
  392.7 8.4 fusion.189
  405.6 6.2 multiply_reduce_fusion.20
  413.6 2.7 fusion.115
  416.3 64.0 %psum.21 = f32[7,7,192]{2,1,0:T(8,128)S(1)} all-reduce(f32[7,7,192]{2,1,0:T(8,128)S(1)} %constant_dynamic-update-slice_fusion.3), channel_id=1, replica_groups=mesh['lon'=32,'lat'=4] {'lon','lat'}, use_global_device_ids=true, to_apply=%region_57.58 | all-reduce | flops 9408 | bytes 75264 | tf_op jit(solution)/shard_map/psum | solution.py:190
  481.5 6.7 collective-permute-start.7
  492.4 59.1 %all-reduce.17.cloned.1.call-done = (f32[192,768]{1,0:T(8,128)}, f32[768,192]{0,1:T(8,128)}) async-done(((f32[192,768]{1,0:T(8,128)}, f32[768,192]{0,1:T(8,128)}), (f32[192,768]{1,0:T(8,128)}, f32[768,192]{0,1:T(8,128)})) %all-reduce.17.cloned.1.call-update) | async-done | bytes 1179664 | tf_op jit(solution)/shard_map/psum | solution.py:190
  555.5 361.6 %all-reduce.15.cloned.1.call-done = bf16[3,2048,192]{2,0,1:T(4,128)(2,1)} async-done(((bf16[3,2048,192]{2,0,1:T(4,128)(2,1)}), bf16[3,2048,192]{2,0,1:T(4,128)(2,1)}) %all-reduce.15.cloned.1.call-update) | async-done | bytes 2359312
  (467 shorter events, 233.0 us)
Async XLA Ops:
  7.2 136.4 %copy-start = (bf16[192,768]{1,0:T(8,128)(2,1)S(1)}, bf16[192,768]{1,0:T(8,128)(2,1)}, u32[]{:S(2)}) copy-start(bf16[192,768]{1,0:T(8,128)(2,1)} %param.21) | copy-start | bytes 884740
  7.2 7.8 copy-start.3
  7.2 98.6 %all-gather.2.cloned.1.call-start = ((), (), s32[]{:S(2)}) async-start(), calls=%async_computation | async-start | bytes 6488064 | tf_op jit(solution)/shard_map/all_gather | solution.py:112
  10.0 541.6 %all-reduce.17.cloned.1.call-start = ((), (), s32[]{:S(2)}) async-start(), calls=%async_computation.2 | async-start | bytes 2359296 | tf_op jit(solution)/shard_map/psum | solution.py:190
  10.0 7.3 collective-permute-start
  10.1 7.3 collective-permute-start.1
  13.1 13.6 %copy-start.137 = (s32[70]{0:T(128)}, s32[70]{0:T(128)S(1)}, u32[]{:S(2)}) copy-start(s32[70]{0:T(128)S(1)} %fusion.173) | copy-start | bytes 844
  13.7 116.8 %copy-start.15 = (f32[1,1,192]{2,1,0:T(1,128)}, f32[1,1,192]{2,1,0:T(1,128)S(1)}, u32[]{:S(2)}) copy-start(f32[1,1,192]{2,1,0:T(1,128)S(1)} %get-tuple-element.204) | copy-start | bytes 2308
  13.7 116.8 %copy-start.17 = (f32[1,1,192]{2,1,0:T(1,128)}, f32[1,1,192]{2,1,0:T(1,128)S(1)}, u32[]{:S(2)}) copy-start(f32[1,1,192]{2,1,0:T(1,128)S(1)} %get-tuple-element.205) | copy-start | bytes 2308
  13.7 116.8 %copy-start.19 = (f32[1,1,192]{2,1,0:T(1,128)}, f32[1,1,192]{2,1,0:T(1,128)S(1)}, u32[]{:S(2)}) copy-start(f32[1,1,192]{2,1,0:T(1,128)S(1)} %get-tuple-element.206) | copy-start | bytes 2308
  13.7 116.8 %copy-start.21 = (f32[1,1,192]{2,1,0:T(1,128)}, f32[1,1,192]{2,1,0:T(1,128)S(1)}, u32[]{:S(2)}) copy-start(f32[1,1,192]{2,1,0:T(1,128)S(1)} %get-tuple-element.207) | copy-start | bytes 2308
  17.3 9.4 %copy-start.107 = (s32[16,64]{1,0:T(8,128)S(1)}, s32[16,64]{1,0:T(8,128)}, u32[]{:S(2)}) copy-start(s32[16,64]{1,0:T(8,128)} %param.15) | copy-start | bytes 12292
  17.5 14.4 %copy-start.4 = (f32[1024,192]{1,0:T(8,128)S(1)}, f32[1024,192]{1,0:T(8,128)}, u32[]{:S(2)}) copy-start(f32[1024,192]{1,0:T(8,128)} %get-tuple-element.211) | copy-start | bytes 2359300
  17.5 16.9 %collective-permute-start.2 = (bf16[2,22,3,192]{3,2,1,0:T(4,128)(2,1)S(1)}, bf16[2,22,3,192]{3,2,1,0:T(4,128)(2,1)S(1)}, u32[]{:S(2)}, u32[]{:S(2)}) collective-permute-start(bf16[2,22,3,192]{3,2,1,0:T(4,128)(2,1)S(1)} %get-tuple-element.98), channel_id=1, source_target_pairs={{0,4},{4,8},{8,12},{12,16},{16,20},{20,24},{24,28},{28,32},{32,36}... | collective-permute-start | bytes 152072 | tf_op jit(solution)/shard_map/ppermute | solution.py:19
  19.6 14.8 %collective-permute-start.3 = (bf16[2,22,3,192]{3,2,1,0:T(4,128)(2,1)S(1)}, bf16[2,22,3,192]{3,2,1,0:T(4,128)(2,1)S(1)}, u32[]{:S(2)}, u32[]{:S(2)}) collective-permute-start(bf16[2,22,3,192]{3,2,1,0:T(4,128)(2,1)S(1)} %get-tuple-element.99), channel_id=1, source_target_pairs={{4,0},{8,4},{12,8},{16,12},{20,16},{24,20},{28,24},{32,28},{36,32}... | collective-permute-start | bytes 152072 | tf_op jit(solution)/shard_map/ppermute | solution.py:22
  112.8 15.7 %copy-start.9 = (bf16[2,22,3,192]{3,2,1,0:T(4,128)(2,1)S(1)}, bf16[2,22,3,192]{3,2,1,0:T(4,128)(2,1)}, u32[]{:S(2)}) copy-start(bf16[2,22,3,192]{3,2,1,0:T(4,128)(2,1)} %copy-done.8) | copy-start | bytes 152068
  112.8 15.7 %copy-start.139 = (pred[70]{0:T(512)(128)(4,1)S(1)}, pred[70]{0:T(512)(128)(4,1)}, u32[]{:S(2)}) copy-start(pred[70]{0:T(512)(128)(4,1)} %compare_and_fusion) | copy-start | bytes 214
  371.4 108.9 %collective-permute-start.4 = (bf16[3,70,192]{2,1,0:T(8,128)(2,1)}, bf16[3,70,192]{2,1,0:T(8,128)(2,1)S(1)}, u32[]{:S(2)}, u32[]{:S(2)}) collective-permute-start(bf16[3,70,192]{2,1,0:T(8,128)(2,1)} %get-tuple-element.158), channel_id=1, source_target_pairs={{0,1},{1,2},{2,3},{3,0},{4,5},{5,6},{6,7},{7,4},{8,9},{9,10},{10,1... | collective-permute-start | bytes 241928 | tf_op jit(solution)/shard_map/ppermute | solution.py:19
  371.4 108.9 %collective-permute-start.5 = (bf16[3,70,192]{2,1,0:T(8,128)(2,1)S(1)}, bf16[3,70,192]{2,1,0:T(8,128)(2,1)S(1)}, u32[]{:S(2)}, u32[]{:S(2)}) collective-permute-start(bf16[3,70,192]{2,1,0:T(8,128)(2,1)S(1)} %get-tuple-element.159), channel_id=1, source_target_pairs={{1,0},{2,1},{3,2},{0,3},{5,4},{6,5},{7,6},{4,7},{9,8},{10,9},{11,1... | collective-permute-start | bytes 241928 | tf_op jit(solution)/shard_map/ppermute | solution.py:22
  386.2 6.4 copy-start.98
  405.5 511.6 %all-reduce.15.cloned.1.call-start = ((), (), s32[]{:S(2)}) async-start(), calls=%async_computation.1 | async-start | bytes 8388608
  480.4 10.0 %collective-permute-start.6 = (bf16[28,3,192]{2,1,0:T(4,128)(2,1)S(1)}, bf16[28,3,192]{2,1,0:T(4,128)(2,1)S(1)}, u32[]{:S(2)}, u32[]{:S(2)}) collective-permute-start(bf16[28,3,192]{2,1,0:T(4,128)(2,1)S(1)} %get-tuple-element.156), channel_id=1, source_target_pairs={{0,4},{4,8},{8,12},{12,16},{16,20},{20,24},{24,28},{28,32},{32,36}... | collective-permute-start | bytes 96776 | tf_op jit(solution)/shard_map/ppermute | solution.py:19
  481.5 8.9 collective-permute-start.7
  551.6 366.6 %copy-start.7 = (bf16[16,64,192]{2,1,0:T(8,128)(2,1)S(1)}, bf16[16,64,192]{2,1,0:T(8,128)(2,1)}, u32[]{:S(2)}) copy-start(bf16[16,64,192]{2,1,0:T(8,128)(2,1)} %param.14) | copy-start | bytes 1179652
  (134 other events, 426.6 us)
Sparse Core Ops, SparseCore 0:
  11.1 94.7 all-gather.1
  405.6 145.9 all-reduce.16
  554.2 362.8 all-reduce.14
where the time goes:
time: 937 us; the launch traced here: 927 us
  waiting for transfers between devices  468 us (50%)
  other arithmetic  183 us (20%)
  local copies, waits for them, and re-layouts  162 us (17%)
  blocking collectives  64 us (7%)
  starting transfers between devices  20.6 us (2%)
  between operations  16.7 us (2%)
  matrix products  13.3 us (1%)
    unnamed x4, waiting for transfers between devices  362 us
    convert_element_type x49, local copies, waits for them, and re-layouts, shards(): padded[1, row_off:row_off + rows, col_off:col_off + cols]  112 us
    psum x1, blocking collectives, shards(): totals = lax.psum((grad_kernel, grad_win, grad_wout), ('lon', 'lat'))  64 us
    convert_element_type x27, other arithmetic, shards(): padded[1, row_off:row_off + rows, col_off:col_off + cols]  63.9 us
    psum x1, waiting for transfers between devices, shards(): totals = lax.psum((grad_kernel, grad_win, grad_wout), ('lon', 'lat'))  59.1 us
    all_gather x1, waiting for transfers between devices, shards(): band_rows = lax.all_gather(top_rows, 'lon', axis=2, tiled=True)  46.6 us
    convert_element_type x1, other arithmetic, shards(): grad_pad.astype(jnp.bfloat16)  37.4 us
    reduce_sum x3, other arithmetic, shards(): jnp.sum(padded[1, row_off:row_off + rows, col_off:col_off + cols].astype(...  18.9 us
  transfers between devices with their start and end apart: 11, of which 4 were waited for; matrix products, arithmetic and copies ran while one was open for 9% of the time, Pallas kernels for 0%

commit v1 on v0

v1 whole, which is shorter than its diff:
```python
import functools
import math

import jax
import jax.numpy as jnp
from jax import lax
from jax.experimental import pallas as pl
from jax.experimental.pallas import tpu as pltpu
from jax.sharding import PartitionSpec as P

F32 = jnp.float32
BF16 = jnp.bfloat16
MESH = pl.DeviceIdType.MESH

ROWS = 16
COLS = 64
PROWS = 22
WIDE = 80
LO = 128
CH = 192
HID = 768
NLON = 2048
CELLS = ROWS * COLS
CHUNK = 256
PIECE = 80
HALF = 16 * PIECE
QUART = 4 * PIECE
WIN_AT, WOUT_AT, WHI_AT, KER_AT = 0, 1152, 1920, 2304

root_factor = math.sqrt(2.0 / math.pi)
cubic_coef = 0.044715
norm_eps = 1e-06
scale = 1.0 / math.sqrt(64 * NLON)

LAT_AT, LON_AT, FOLD1_AT, FOLD2_AT = 0, 2, 8, 13
FIELD = 21
S0_AT, S1_AT, S2_AT, S3_AT, G1_AT, G2_AT, G3_AT = 42, 43, 46, 49, 52, 55, 58
COPIES = 59


def dot(a, b, dims=((1,), (0,))):
    return lax.dot_general(a, b, (dims, ((), ())), preferred_element_type=F32)


def kernel(
    x_ref, go_ref, mask_ref, partner_ref, dw_ref, dwb_ref, g_ref, lb_ref, win_ref, bin_ref,
    wout_ref, bout_ref, ls_ref,
    outa_ref, gs_ref, gk_ref, gwin_ref, gwout_ref,
    pd, pz, xb, zb, sx, sz, rlx, rlz, rcx, rcz, fx1, fz1, vx, vz, fx2, fz2,
    dp, mb, kt, wa, wb, gw, gwo, flat, r0, hb, r1, q, r2, r3, ag, ssem, rsem,
):
    lon = lax.axis_index("lon")
    lat = lax.axis_index("lat")
    top = lat == 3
    xx, yh, zz = lon // 8, (lon // 4) % 2, lon % 4
    yl, core = lat // 2, lat % 2
    yy = yh * 2 + yl

    def lon_of(step):
        return (lon + step + 64) % 32

    mate = (lon, lat + 1 - 2 * core)

    def first_peer(k):
        far_x = ((xx + k) % 4) * 8 + yh * 4 + zz
        far_z = xx * 8 + yh * 4 + (zz + k) % 4
        return (jnp.where(core == 0, far_x, far_z), lat)

    def second_peer(k):
        far_x = ((xx + k) % 4) * 8 + yh * 4 + zz
        far_z = xx * 8 + yh * 4 + (zz + k) % 4
        return (jnp.where(core == 0, far_z, far_x), lat)

    def third_peer(k):
        far = (yy + k) % 4
        return (xx * 8 + (far // 2) * 4 + zz, (far % 2) * 2 + core)

    c1 = jnp.where(core == 0, xx, zz)
    c2 = jnp.where(core == 0, zz, xx)

    def remote(src, dst, i, peer):
        return pltpu.make_async_remote_copy(
            src_ref=src, dst_ref=dst, send_sem=ssem.at[i], recv_sem=rsem.at[i],
            device_id={"lon": peer[0], "lat": peer[1]}, device_id_type=MESH,
        )

    barrier = pltpu.get_barrier_semaphore()

    def greet(peer):
        pl.semaphore_signal(
            barrier, inc=1, device_id={"lon": peer[0], "lat": peer[1]}, device_id_type=MESH
        )

    greet(mate)
    for k in (1, 2, 3):
        greet(first_peer(k))
        greet(second_peer(k))
        greet(third_peer(k))
    for side in (-1, 1):
        greet((lon_of(side), lat))
    for dl in (-1, 1):
        @pl.when((lat + dl >= 0) & (lat + dl <= 3))
        def _():
            for side in (-1, 0, 1):
                greet((lon_of(side), lat + dl))

    @pl.when(top)
    def _():
        for k in range(1, 6):
            greet((lon_of(k), lat))
        for k in range(8):
            greet((lon_of(31 - 2 * lon + 4 * k), lat))

    def at(plane, row, col):
        return (plane * PROWS + row) * WIDE + col

    def spread(r, carry):
        a = x_ref[0, r].astype(F32)
        b = x_ref[1, r].astype(F32)
        mix = jnp.concatenate([a[:, LO:], b[:, LO:]], axis=1)
        for plane, v in enumerate((a[:, :LO], b[:, :LO], mix)):
            pd[pl.ds(pl.multiple_of(at(plane, 3 + r, 8), 8), COLS), :] = v
            xb[plane, r] = v.astype(BF16)
        return carry

    lax.fori_loop(0, ROWS, spread, 0)

    def pack(field, send, planes):
        for plane in range(planes):
            for k in range(3):
                send[0, plane, k] = field[pl.ds(at(plane, 3, 8 + k), ROWS, stride=WIDE), :].astype(BF16)
                send[1, plane, k] = field[pl.ds(at(plane, 3, 69 + k), ROWS, stride=WIDE), :].astype(BF16)

    pack(pd, sx, 3)

    def clear_south(field, planes):
        for plane in range(planes):
            field[pl.ds(at(plane, 0, 0), 3 * WIDE), :] = jnp.zeros((3 * WIDE, LO), F32)

    clear_south(pd, 3)
    clear_south(pz, 2)

    peers = 12 + jnp.where(lat > 0, 3, 0) + jnp.where(lat < 3, 3, 0) + jnp.where(top, 13, 0)
    pl.semaphore_wait(barrier, peers)

    def lat_copies(base, block, got):
        return (
            (lat < 3, remote(block.at[:, 13:16], got.at[0], base + LAT_AT, (lon, lat + 1))),
            (lat > 0, remote(block.at[:, 0:3], got.at[1], base + LAT_AT + 1, (lon, lat - 1))),
        )

    def lon_copies(base, send, got):
        found = []
        for side in range(2):
            for slot in range(3):
                dl = 1 - slot
                found.append((
                    (lat + dl >= 0) & (lat + dl <= 3),
                    remote(
                        send.at[1 - side], got.at[side, slot], base + LON_AT + 3 * side + slot,
                        (lon_of(1 - 2 * side), lat + dl),
                    ),
                ))
        return found

    def lon_arrives(slot):
        return (lat + slot - 1 >= 0) & (lat + slot - 1 <= 3)

    def fold1_copies(base, block, got):
        return [
            remote(block.at[:, 13:16], got.at[k], base + FOLD1_AT + k - 1, (lon_of(-k), lat))
            for k in range(1, 6)
        ]

    def fold2_copies(base, window, got):
        return [
            remote(window, got.at[k], base + FOLD2_AT + k, (lon_of(31 - 2 * lon + 4 * k), lat))
            for k in range(8)
        ]

    def start_halo(base, block, send, rl, rc, f1):
        for cond, copy in lon_copies(base, send, rc):
            pl.when(cond)(copy.start)
        for cond, copy in lat_copies(base, block, rl):
            pl.when(cond)(copy.start)

        @pl.when(top)
        def _():
            for copy in fold1_copies(base, block, f1):
                copy.start()

    def finish_halo(base, field, planes, block, send, rl, rc):
        lats = lat_copies(base, block, rl)
        for way, (arrives, row) in enumerate(((lat > 0, 0), (lat < 3, 19))):
            @pl.when(arrives)
            def _(way=way, row=row):
                lats[way][1].wait_recv()
                for plane in range(planes):
                    for r in range(3):
                        field[pl.ds(at(plane, row + r, 8), COLS), :] = rl[way, plane, r].astype(F32)
        lons = lon_copies(base, send, rc)
        for side in range(2):
            col = 5 if side == 0 else 72
            for slot in range(3):
                @pl.when(lon_arrives(slot))
                def _(side=side, slot=slot, col=col):
                    lons[3 * side + slot][1].wait_recv()
                    for plane in range(planes):
                        for k in range(3):
                            v = rc[side, slot, plane, k].astype(F32)
                            if slot == 1:
                                field[pl.ds(at(plane, 3, col + k), ROWS, stride=WIDE), :] = v
                            else:
                                for r in range(3):
                                    row = r if slot == 0 else 19 + r
                                    own = 13 + r if slot == 0 else r
                                    field[pl.ds(at(plane, row, col + k), 1), :] = v[own:own + 1]

    begin = lax.rem(partner_ref[0] + (NLON - 2), NLON)
    offset = lax.rem(begin, COLS)
    near = lax.rem(lax.div(begin, COLS), 4)
    far = lax.div(begin, 4 * COLS)

    def middle_fold(base, planes, block, f1, window, f2):
        for copy in fold1_copies(base, block, f1):
            copy.wait_recv()
        f1[0] = block[:, 13:16]
        slot_at = lax.broadcasted_iota(jnp.int32, (WIDE, 3 * COLS), 0)
        from_at = lax.broadcasted_iota(jnp.int32, (WIDE, 3 * COLS), 1)
        pick = jnp.where(from_at + slot_at == offset + 74, 1.0, 0.0).astype(BF16)
        for plane in range(planes):
            for r in range(3):
                three = jnp.concatenate([f1[near + c, plane, r] for c in range(3)], axis=0)
                window[plane, r] = dot(pick, three).astype(BF16)
        for copy in fold2_copies(base, window, f2):
            copy.start()

    def finish_fold(base, field, planes, window, f2):
        for copy in fold2_copies(base, window, f2):
            copy.wait_recv()
        for plane in range(planes):
            for k in range(3):
                field[pl.ds(at(plane, 19 + k, 0), WIDE), :] = f2[far, plane, 2 - k].astype(F32)

    def close_field(base, block, send, rl, rc, f1, window, f2):
        for cond, copy in lat_copies(base, block, rl):
            pl.when(cond)(copy.wait_send)
        for cond, copy in lon_copies(base, send, rc):
            pl.when(cond)(copy.wait_send)

        @pl.when(top)
        def _():
            for copy in fold1_copies(base, block, f1):
                copy.wait_send()
            for copy in fold2_copies(base, window, f2):
                copy.wait_send()

    start_halo(0, xb, sx, rlx, rcx, fx1)

    lane = lax.broadcasted_iota(jnp.int32, (1, LO), 1)
    upper = lane >= 64

    def table(a, carry):
        low, high = dw_ref[a][:, :LO], dw_ref[a][:, LO:]
        mix = jnp.concatenate([high, high], axis=1)
        rlow, rhigh = dw_ref[6 - a][:, :LO], dw_ref[6 - a][:, LO:]
        rmix = jnp.concatenate([rhigh, rhigh], axis=1)
        for b in range(7):
            for kind, (v, w) in enumerate(((low, rlow), (mix, rmix))):
                straight = jnp.broadcast_to(v[b:b + 1], (8, LO))
                turned = jnp.broadcast_to(w[6 - b:7 - b], (8, LO))
                kt[kind, a * 7 + b] = straight
                kt[2 + kind, a * 7 + b] = turned
                kt[4 + kind, a * 7 + b] = jnp.where(top, straight, turned)
        return carry

    lax.fori_loop(0, 7, table, 0)
    wa[0:192] = win_ref[...]
    wa[192:256] = jnp.zeros((64, HID), BF16)
    wb[0:128] = win_ref[0:128]
    wb[128:192] = jnp.zeros((64, HID), BF16)
    wb[192:256] = win_ref[128:192]
    eye = jnp.where(
        lax.broadcasted_iota(jnp.int32, (COLS, COLS), 0) == lax.broadcasted_iota(jnp.int32, (COLS, COLS), 1),
        1.0, 0.0,
    ).astype(BF16)
    mask_t = dot(eye, mask_ref[...].astype(F32).astype(BF16), ((1,), (1,))).astype(BF16)
    for r in range(ROWS):
        one = jnp.where(lax.broadcasted_iota(jnp.int32, (ROWS, LO), 0) == r, 1.0, 0.0).astype(BF16)
        mb[r * COLS:(r + 1) * COLS] = dot(mask_t, one)
    gw[...] = jnp.zeros_like(gw)
    gwo[...] = jnp.zeros_like(gwo)

    zero64 = jnp.zeros((1, 64), F32)

    def halves(ref, state):
        v = ref[...]
        high = v[:, LO:]
        parts = [high, zero64] if state == 0 else [zero64, high]
        return v[:, :LO], jnp.concatenate(parts, axis=1)

    def conv(field, plane, c, half, tab, tab_last):
        base = at(plane, 4 * c, 32 * half + 5)
        acc = [[jnp.zeros((8, LO), F32) for _ in range(4)] for _ in range(4)]
        for p in range(10):
            for b in range(7):
                use = tab_last if p >= 7 else tab
                ks = {r: kt[use, (p - r) * 7 + b] for r in range(4) if 0 <= p - r <= 6}
                for t in range(4):
                    v = field[pl.ds(base + p * WIDE + 8 * t + b, 8), :]
                    for r, kv in ks.items():
                        acc[r][t] = acc[r][t] + kv * v
        return acc

    def norm(c, state):
        here = pl.ds(pl.multiple_of(c * CHUNK, CHUNK), CHUNK)
        keep = upper if state == 1 else jnp.logical_not(upper)
        blo, bhi = halves(dwb_ref, state)
        glo, ghi = halves(g_ref, state)
        llo, lhi = halves(lb_ref, state)
        lo = dp[state, here] + blo
        hi = jnp.where(keep, dp[2, here] + bhi, 0.0)
        mean = jnp.sum(lo + hi, axis=1, keepdims=True) * (1.0 / CH)
        lo = lo - mean
        hi = jnp.where(keep, hi - mean, 0.0)
        inv = lax.rsqrt(jnp.sum(lo * lo + hi * hi, axis=1, keepdims=True) * (1.0 / CH) + norm_eps)
        nlo, nhi = lo * inv, hi * inv
        low = jnp.concatenate(
            [(nlo * glo + llo).astype(BF16), (nhi * ghi + lhi).astype(BF16)], axis=1
        )
        return low, nlo, nhi, inv, glo, ghi, keep

    def forward_chunk(c):
        low = norm(c, 0)[0]
        mixed = jnp.broadcast_to(bout_ref[...], (CHUNK, CH))
        for s in range(3):
            cut = slice(256 * s, 256 * s + 256)
            u = dot(low, wa[:, cut]) + bin_ref[:, cut]
            t = jnp.tanh(u * (root_factor + (root_factor * cubic_coef) * (u * u)))
            act = (u * (0.5 + 0.5 * t)).astype(BF16)
            mixed = mixed + dot(act, wout_ref[cut])
        mixed = mixed * ls_ref[...]
        here = pl.ds(pl.multiple_of(c * CHUNK, CHUNK), CHUNK)
        m = mb[here]
        mm = jnp.concatenate([m, m[:, :64]], axis=1)
        for r in range(4):
            cut = slice(64 * r, 64 * r + 64)
            outa_ref[4 * c + r] = (x_ref[0, 4 * c + r].astype(F32) + mm[cut] * mixed[cut]).astype(BF16)

    def backward_chunk(c):
        low, nlo, nhi, inv, glo, ghi, keep = norm(c, 1)
        here = pl.ds(pl.multiple_of(c * CHUNK, CHUNK), CHUNK)
        m = mb[here]
        mm = jnp.concatenate([m, m[:, :64]], axis=1)
        go = jnp.concatenate([go_ref[4 * c + r] for r in range(4)], axis=0).astype(F32)
        gl = (mm * (ls_ref[...] * go)).astype(BF16)
        gn = jnp.zeros((CHUNK, 256), F32)
        for s in range(3):
            cut = slice(256 * s, 256 * s + 256)
            u = dot(low, wb[:, cut]) + bin_ref[:, cut]
            u2 = u * u
            t = jnp.tanh(u * (root_factor + (root_factor * cubic_coef) * u2))
            half = 0.5 + 0.5 * t
            value = u * half
            slope = half + value * (1.0 - t) * (root_factor + (3.0 * root_factor * cubic_coef) * u2)
            act = value.astype(BF16)
            gwo[cut] += dot(act, gl, ((0,), (0,)))
            gh = (dot(gl, wout_ref[cut], ((1,), (1,))) * slope).astype(BF16)
            gw[:, cut] += dot(low, gh, ((0,), (0,)))
            gn = gn + dot(gh, wb[:, cut], ((1,), (1,)))
        nl, nh = gn[:, :LO] * glo, gn[:, LO:] * ghi
        one = jnp.sum(nl + nh, axis=1, keepdims=True) * (1.0 / CH)
        two = jnp.sum(nl * nlo + nh * nhi, axis=1, keepdims=True) * (1.0 / CH)
        zl = inv * (nl - one - nlo * two)
        zh = jnp.where(keep, inv * (nh - one - nhi * two), 0.0)
        for plane, v in enumerate((zl, zh)):
            for r in range(4):
                cut = slice(64 * r, 64 * r + 64)
                pz[pl.ds(pl.multiple_of(at(plane, 3 + 4 * c + r, 8), 8), COLS), :] = v[cut]
                zb[plane, 4 * c + r] = v[cut].astype(BF16)

    finish_halo(0, pd, 3, xb, sx, rlx, rcx)

    @pl.when(top)
    def _():
        middle_fold(0, 3, xb, fx1, vx, fx2)

    def first_pass(c, carry):
        @pl.when(top & (c == 3))
        def _():
            finish_fold(0, pd, 3, vx, fx2)

        def sweep(i, carry):
            plane, half = i // 2, i % 2
            kind = plane // 2
            acc = conv(pd, plane, c, half, kind, kind)
            for r in range(4):
                for t in range(4):
                    cell = pl.multiple_of(c * CHUNK + r * COLS + half * 32 + 8 * t, 8)
                    dp[plane, pl.ds(cell, 8)] = acc[r][t]
            return carry

        lax.fori_loop(0, 6, sweep, 0)
        backward_chunk(c)
        return carry

    lax.fori_loop(0, 4, first_pass, 0)

    pack(pz, sz, 2)
    start_halo(FIELD, zb, sz, rlz, rcz, fz1)

    for plane in range(2):
        for rows in ((0, 1, 2, 3), (4, 5, 6)):
            def add_row(i, acc, plane=plane, rows=rows):
                acc = list(acc)
                for t in range(8):
                    z = pz[pl.ds(pl.multiple_of(at(plane, 3 + i, 8 + 8 * t), 8), 8), :]
                    for n, a in enumerate(rows):
                        for b in range(7):
                            v = pd[pl.ds(at(1 + plane, i + a, 5 + 8 * t + b), 8), :]
                            acc[n * 7 + b] = acc[n * 7 + b] + v * z
                return tuple(acc)

            acc = lax.fori_loop(
                0, ROWS, add_row, tuple(jnp.zeros((8, LO), F32) for _ in range(7 * len(rows)))
            )
            for n, a in enumerate(rows):
                for b in range(7):
                    line = KER_AT + plane * 56 + a * 7 + b
                    flat[line:line + 1] = jnp.sum(acc[n * 7 + b], axis=0, keepdims=True)
        flat[KER_AT + plane * 56 + 49:KER_AT + plane * 56 + 56] = jnp.zeros((7, LO), F32)
    flat[KER_AT + 112:2560] = jnp.zeros((2560 - KER_AT - 112, LO), F32)

    for s in range(6):
        cut = slice(128 * s, 128 * s + 128)
        flat[WIN_AT + 192 * s:WIN_AT + 192 * s + 128] = gw[0:128, cut]
        flat[WIN_AT + 192 * s + 128:WIN_AT + 192 * s + 192] = gw[192:256, cut]
    flat[WOUT_AT:WOUT_AT + HID] = gwo[:, :LO]
    flat[WHI_AT:WHI_AT + 384] = jnp.concatenate([gwo[0:384, LO:], gwo[384:768, LO:]], axis=1)

    def half_at(which):
        return pl.ds(pl.multiple_of(which * HALF, 8), HALF)

    s0 = remote(flat.at[half_at(1 - core)], r0, S0_AT, mate)

    def s1(k):
        return remote(hb.at[(c1 + k) % 4], r1.at[k - 1], S1_AT + k - 1, first_peer(k))

    def s2(k):
        return remote(q.at[(c2 + k) % 4], r2.at[k - 1], S2_AT + k - 1, second_peer(k))

    def s3(k):
        return remote(r3.at[yy], r3.at[yy], S3_AT + k - 1, third_peer(k))

    def s3_from(k):
        return remote(r3.at[yy], r3.at[(yy + 4 - k) % 4], S3_AT + k - 1, third_peer(k))

    def g1(k):
        return remote(ag.at[core, c1, c2], ag.at[core, c1, c2], G1_AT + k - 1, second_peer(k))

    def g1_from(k):
        return remote(ag.at[core, c1, c2], ag.at[core, c1, (c2 + 4 - k) % 4], G1_AT + k - 1, second_peer(k))

    def g2(k):
        return remote(ag.at[core, c1], ag.at[core, c1], G2_AT + k - 1, first_peer(k))

    def g2_from(k):
        return remote(ag.at[core, c1], ag.at[core, (c1 + 4 - k) % 4], G2_AT + k - 1, first_peer(k))

    g3 = remote(ag.at[core], ag.at[core], G3_AT, mate)
    g3_from = remote(ag.at[core], ag.at[1 - core], G3_AT, mate)

    s0.start()

    def second_pass(step, carry):
        @pl.when(step == 1)
        def _():
            finish_halo(FIELD, pz, 2, zb, sz, rlz, rcz)
            s0.wait_recv()
            for i in range(4):
                part = pl.ds(pl.multiple_of(core * HALF + i * QUART, 8), QUART)
                total = flat[part] + r0[i * QUART:(i + 1) * QUART]
                flat[part] = total
                hb[i] = total.astype(BF16)
            for k in (1, 2, 3):
                s1(k).start()

        @pl.when((step == 1) & top)
        def _():
            middle_fold(FIELD, 2, zb, fz1, vz, fz2)

        @pl.when(step == 2)
        def _():
            for k in (1, 2, 3):
                s1(k).wait_recv()
            total = flat[pl.ds(pl.multiple_of(core * HALF + c1 * QUART, 8), QUART)]
            for k in range(3):
                total = total + r1[k].astype(F32)
            for i in range(4):
                q[i] = total[i * PIECE:(i + 1) * PIECE]
            for k in (1, 2, 3):
                s2(k).start()

        @pl.when(step == 3)
        def _():
            for k in (1, 2, 3):
                s2(k).wait_recv()
            r3[yy] = q[c2] + r2[0] + r2[1] + r2[2]
            for k in (1, 2, 3):
                s3(k).start()

        @pl.when(step == 4)
        def _():
            for k in (1, 2, 3):
                s3_from(k).wait_recv()
            ag[core, c1, c2] = ((r3[0] + r3[1] + r3[2] + r3[3]) * scale).astype(BF16)
            for k in (1, 2, 3):
                g1(k).start()

        @pl.when(step == 5)
        def _():
            for k in (1, 2, 3):
                g1_from(k).wait_recv()
            for k in (1, 2, 3):
                g2(k).start()

        @pl.when(step == 6)
        def _():
            for k in (1, 2, 3):
                g2_from(k).wait_recv()
            g3.start()

        @pl.when((step == 7) & top)
        def _():
            finish_fold(FIELD, pz, 2, vz, fz2)

        @pl.when(step < 4)
        def _():
            forward_chunk(step)

        @pl.when(step >= 4)
        def _():
            c = step - 4
            last = jnp.where(c == 3, 4, 2)

            def sweep(half, carry):
                at_col = pl.ds(pl.multiple_of(32 * half, 32), 32)
                acc_lo = conv(pz, 0, c, half, 2, last)
                for r in range(4):
                    low = jnp.concatenate(acc_lo[r], axis=0)
                    go = go_ref[4 * c + r, at_col, :].astype(F32)
                    gs_ref[4 * c + r, at_col, 0:LO] = low + go[:, :LO]
                acc_hi = conv(pz, 1, c, half, 3, last + 1)
                for r in range(4):
                    high = jnp.concatenate(acc_hi[r], axis=0)
                    go = go_ref[4 * c + r, at_col, :].astype(F32)
                    gs_ref[4 * c + r, at_col, LO:CH] = high[:, 64:] + go[:, LO:]
                return carry

            lax.fori_loop(0, 2, sweep, 0)

        return carry

    lax.fori_loop(0, 8, second_pass, 0)

    g3_from.wait_recv()

    def part_of(start, size):
        first, end = start // PIECE, -(-(start + size) // PIECE)
        found = [ag[i // 16, (i // 4) % 4, i % 4] for i in range(first, end)]
        return jnp.concatenate(found, axis=0)[start - first * PIECE:start - first * PIECE + size].astype(F32)

    for s in range(6):
        gwin_ref[:, 128 * s:128 * s + 128] = part_of(WIN_AT + 192 * s, 192)
    gwout_ref[:, 0:LO] = part_of(WOUT_AT, HID)
    both = part_of(WHI_AT, 384)
    gwout_ref[0:384, LO:CH] = both[:, :64]
    gwout_ref[384:768, LO:CH] = both[:, 64:]
    klow = part_of(KER_AT, 56)
    khigh = part_of(KER_AT + 56, 56)
    for a in range(7):
        gk_ref[a, :, 0:LO] = klow[7 * a:7 * a + 7]
        gk_ref[a, :, LO:CH] = khigh[7 * a:7 * a + 7, 64:]

    close_field(0, xb, sx, rlx, rcx, fx1, vx, fx2)
    close_field(FIELD, zb, sz, rlz, rcz, fz1, vz, fz2)
    s0.wait_send()
    for k in (1, 2, 3):
        s1(k).wait_send()
        s2(k).wait_send()
        s3(k).wait_send()
        g1(k).wait_send()
        g2(k).wait_send()
    g3.wait_send()


def shards(states, grad_out, land_mask, partner, dw_kernel, dw_bias, ln_gain, ln_bias, w_in, b_in,
           w_out, b_out, layer_scale):
    def row(v):
        return v.reshape(1, v.shape[0])

    vmem = pl.BlockSpec(memory_space=pltpu.VMEM)
    smem = pl.BlockSpec(memory_space=pltpu.SMEM)

    def buf(*shape, dtype=F32):
        return pltpu.VMEM(shape, dtype)

    scratch = [
        buf(3 * PROWS * WIDE, LO), buf(2 * PROWS * WIDE, LO),
        buf(3, ROWS, COLS, LO, dtype=BF16), buf(2, ROWS, COLS, LO, dtype=BF16),
        buf(2, 3, 3, ROWS, LO, dtype=BF16), buf(2, 2, 3, ROWS, LO, dtype=BF16),
        buf(2, 3, 3, COLS, LO, dtype=BF16), buf(2, 2, 3, COLS, LO, dtype=BF16),
        buf(2, 3, 3, 3, ROWS, LO, dtype=BF16), buf(2, 3, 2, 3, ROWS, LO, dtype=BF16),
        buf(6, 3, 3, COLS, LO, dtype=BF16), buf(6, 2, 3, COLS, LO, dtype=BF16),
        buf(3, 3, WIDE, LO, dtype=BF16), buf(2, 3, WIDE, LO, dtype=BF16),
        buf(8, 3, 3, WIDE, LO, dtype=BF16), buf(8, 2, 3, WIDE, LO, dtype=BF16),
        buf(3, CELLS, LO), buf(CELLS, LO), buf(6, 49, 8, LO),
        buf(256, HID, dtype=BF16), buf(256, HID, dtype=BF16),
        buf(256, HID), buf(HID, CH), buf(2 * HALF, LO),
        buf(HALF, LO), buf(4, QUART, LO, dtype=BF16), buf(3, QUART, LO, dtype=BF16),
        buf(4, PIECE, LO), buf(3, PIECE, LO), buf(4, PIECE, LO),
        buf(2, 4, 4, PIECE, LO, dtype=BF16),
        pltpu.SemaphoreType.DMA((COPIES,)), pltpu.SemaphoreType.DMA((COPIES,)),
    ]
    outs = (
        jax.ShapeDtypeStruct((ROWS, COLS, CH), BF16),
        jax.ShapeDtypeStruct((ROWS, COLS, CH), F32),
        jax.ShapeDtypeStruct((7, 7, CH), F32),
        jax.ShapeDtypeStruct((CH, HID), F32),
        jax.ShapeDtypeStruct((HID, CH), F32),
    )
    return pl.pallas_call(
        kernel,
        out_shape=outs,
        in_specs=[vmem, vmem, vmem, smem] + [vmem] * 9,
        out_specs=(vmem,) * 5,
        scratch_shapes=scratch,
        compiler_params=pltpu.CompilerParams(
            collective_id=0, has_side_effects=True, vmem_limit_bytes=56 * 1024 * 1024
        ),
        name="block",
    )(
        states, grad_out, land_mask, partner, dw_kernel, row(dw_bias), row(ln_gain), row(ln_bias),
        w_in, row(b_in), w_out, row(b_out), row(layer_scale),
    )


def solution(mesh):
    placed = (
        P(None, "lat", "lon", None), P("lat", "lon", None), P("lat", "lon"),
        P(), P(), P(), P(), P(), P(), P(), P(), P(), P(),
    )
    return jax.shard_map(
        shards,
        mesh=mesh,
        in_specs=placed,
        out_specs=(P("lat", "lon", None), P("lat", "lon", None), P(), P(), P()),
        check_vma=False,
    )
```

time: 937 us -> 94.2 us (0.10)
  the two profiles are of different devices: /device:TPU:0 before, /device:TPU:1 now
where the time goes in v1:
time: 94.2 us; the launch traced here: 93.9 us
  Pallas kernels  83.5 us (89%)
  local copies, waits for them, and re-layouts  9.72 us (10%)
    pallas_call x1, Pallas kernels, shards(): pl.pallas_call(kernel, out_shape=outs, in_specs=[vmem, vmem, vmem, smem]...  83.5 us
    unnamed x13, local copies, waits for them, and re-layouts  6.86 us
    pallas_call x1, local copies, waits for them, and re-layouts, shards(): pl.pallas_call(kernel, out_shape=outs, in_specs=[vmem, vmem, vmem, smem]...  2.29 us

profile of v1, /device:TPU:1, one launch (start us, length us, event | category | flops | bytes accessed | tf_op | source)
XLA Modules:
  0.0 93.9 jit_solution(12225336531349727024)
XLA Ops:
  0.6 0.0 copy-start.3
  0.6 0.7 copy-done.3
  1.3 0.6 reshape.31.bin_ref
  1.9 1.9 %copy.18.wout_ref = bf16[768,192]{1,0:T(8,128)(2,1)} copy(bf16[768,192]{0,1:T(8,128)(2,1)} %param.23) | data formatting | bytes 589824 | tf_op args[10]
  3.8 83.5 %block.1 = (bf16[16,64,192]{2,1,0:T(8,128)(2,1)}, f32[16,64,192]{2,1,0:T(8,128)}, f32[7,7,192]{2,1,0:T(8,128)}, f32[192,768]{1,0:T(8,128)}, f32[768,192]{1,0:T(8,128)}) custom-call(bf16[2,16,64,192]{3,2,1,0:T(8,128)(2,1)} %x_ref.1, bf16[16,64,192]{2,1,0:T(8,128)(2,1)} %go_ref.1, s32[16,64]{1,0:T(8,128)} %mask_ref.1, s32[2048]{0:T(1024)} %partner_ref.1, ...), custom_call_target="tpu_custom_call" | custom-call | tf_op jit(solution)/shard_map/block/pallas_call | solution.py:632
  87.3 0.0 copy-start
  87.3 2.3 %copy.19 = f32[768,192]{0,1:T(8,128)} copy(f32[768,192]{1,0:T(8,128)} %get-tuple-element.9) | data formatting | bytes 1179648 | tf_op jit(solution)/shard_map/block/pallas_call | solution.py:632
  89.6 1.9 %copy.24 = bf16[16,64,192]{2,1,0:T(8,128)(2,1)} copy(bf16[16,64,192]{2,1,0:T(8,128)(2,1)} %get-tuple-element.15) | data formatting | bytes 786432
  91.5 0.0 copy-done
  91.5 0.0 copy-start.2
  91.5 0.0 copy-start.1
  91.5 1.0 %copy.25 = f32[16,64,192]{2,1,0:T(8,128)} copy(f32[16,64,192]{2,1,0:T(8,128)S(1)} %copy-done) | data formatting | bytes 1572864
  92.5 0.0 copy-done.2
  92.5 0.6 copy.26
  93.1 0.0 copy-done.1
  93.1 0.8 copy.27
Async XLA Ops:
  0.6 0.7 copy-start.3
  87.3 4.2 %copy-start = (f32[16,64,192]{2,1,0:T(8,128)S(1)}, f32[16,64,192]{2,1,0:T(8,128)}, u32[]{:S(2)}) copy-start(f32[16,64,192]{2,1,0:T(8,128)} %get-tuple-element.16) | copy-start | bytes 2359300
  91.5 1.0 %copy-start.2 = (f32[7,7,192]{2,1,0:T(8,128)S(1)}, f32[7,7,192]{2,1,0:T(8,128)}, u32[]{:S(2)}) copy-start(f32[7,7,192]{2,1,0:T(8,128)} %get-tuple-element.17) | copy-start | bytes 112900
  91.5 1.6 %copy-start.1 = (f32[192,768]{1,0:T(8,128)S(1)}, f32[192,768]{1,0:T(8,128)}, u32[]{:S(2)}) copy-start(f32[192,768]{1,0:T(8,128)} %get-tuple-element.18) | copy-start | bytes 1769476

commit v2 on v1

v2 whole, which is shorter than its diff:
```python
import functools
import math

import jax
import jax.numpy as jnp
from jax import lax
from jax.experimental import pallas as pl
from jax.experimental.pallas import tpu as pltpu
from jax.sharding import PartitionSpec as P

F32 = jnp.float32
BF16 = jnp.bfloat16
MESH = pl.DeviceIdType.MESH

ROWS = 16
COLS = 64
PROWS = 22
WIDE = 80
LO = 128
CH = 192
HID = 768
NLON = 2048
CELLS = ROWS * COLS
CHUNK = 256
PIECE = 80
HALF = 16 * PIECE
QUART = 4 * PIECE
WIN_AT, WOUT_AT, KER_AT = 0, 1152, 2304

root_factor = math.sqrt(2.0 / math.pi)
cubic_coef = 0.044715
norm_eps = 1e-06
scale = 1.0 / math.sqrt(64 * NLON)

LAT_AT, LON_AT, FIELD = 0, 2, 8
FOLD_B, FOLD_A, FOLD_Z, ROUND = 16, 30, 44, 6
S0_AT, S1_AT, S3_AT, G1_AT, G3_AT = 58, 59, 74, 77, 92
COPIES = 93


def dot(a, b, dims=((1,), (0,))):
    return lax.dot_general(a, b, (dims, ((), ())), preferred_element_type=F32)


def kernel(
    x_in, go_in, mask_in, partner_in, dw_in, dwb_in, g_in, lb_in, win_in, bin_in,
    wout_in, bout_in, ls_in,
    outa_ref, gs_ref, gk_ref, gwin_ref, gwout_ref,
    x_ref, go_ref, mask_ref, partner_ref, dw_ref, dwb_ref, g_ref, lb_ref, win_ref, bin_ref,
    wout_ref, bout_ref, ls_ref, load_sem,
    pd, pz, xb, zb, sx, sz, rlx, rlz, rcx, rcz, fb1, fa1, fz1, vb, va, vz, fb2, fya, fyz, fxa, fxz,
    dp, mb, kt, wa, wb, gw, gwo, gka, flat, b0, r0, hb, r1, r3, ag, ssem, rsem,
):
    lon = lax.axis_index("lon")
    lat = lax.axis_index("lat")
    top = lat == 3
    xx, yh, zz = lon // 8, (lon // 4) % 2, lon % 4
    yl, core = lat // 2, lat % 2
    yy = yh * 2 + yl

    def lon_of(step):
        return (lon + step + 64) % 32

    mate = (lon, lat + 1 - 2 * core)

    def plane_peer(m):
        return (((xx + m // 4) % 4) * 8 + yh * 4 + (zz + m % 4) % 4, lat)

    def third_peer(k):
        far = (yy + k) % 4
        return (xx * 8 + (far // 2) * 4 + zz, (far % 2) * 2 + core)

    place = xx * 4 + zz

    def place_of(m):
        return ((xx + m // 4) % 4) * 4 + (zz + m % 4) % 4

    block8 = lon // 4
    mirror = lon + 3 - 2 * zz
    own1 = 2 * zz - 3
    own2 = (2 * block8 + 1) % 8

    def mirror_of(v):
        return v + 3 - 2 * (v % 4)

    def fold1_to(k):
        return mirror_of(lon_of(-k))

    def fold1_from(k):
        return (mirror + k) % 32

    def fold2_peer(k):
        return ((7 - block8 + k) % 8) * 4 + zz

    def remote(src, dst, i, peer):
        return pltpu.make_async_remote_copy(
            src_ref=src, dst_ref=dst, send_sem=ssem.at[i], recv_sem=rsem.at[i],
            device_id={"lon": peer[0], "lat": peer[1]}, device_id_type=MESH,
        )

    barrier = pltpu.get_barrier_semaphore()

    def greet(peer):
        pl.semaphore_signal(
            barrier, inc=1, device_id={"lon": peer[0], "lat": peer[1]}, device_id_type=MESH
        )

    greet(mate)
    for m in range(1, 16):
        greet(plane_peer(m))
    for k in (1, 2, 3):
        greet(third_peer(k))
    for side in (-1, 1):
        greet((lon_of(side), lat))
    for dl in (-1, 1):
        @pl.when((lat + dl >= 0) & (lat + dl <= 3))
        def _():
            for side in (-1, 0, 1):
                greet((lon_of(side), lat + dl))

    @pl.when(top)
    def _():
        for k in range(6):
            @pl.when(k != own1)
            def _(k=k):
                greet((fold1_from(k), lat))
        for k in range(8):
            @pl.when(k != own2)
            def _(k=k):
                greet((fold2_peer(k), lat))

    ins = (x_in, go_in, mask_in, partner_in, dw_in, dwb_in, g_in, lb_in, win_in, bin_in,
           wout_in, bout_in, ls_in)
    held = (x_ref, go_ref, mask_ref, partner_ref, dw_ref, dwb_ref, g_ref, lb_ref, win_ref, bin_ref,
            wout_ref, bout_ref, ls_ref)
    loads = [pltpu.make_async_copy(a, b, load_sem.at[i]) for i, (a, b) in enumerate(zip(ins, held))]
    for load in loads:
        load.start()
    loads[0].wait()

    def at(plane, row, col):
        return (plane * PROWS + row) * WIDE + col

    def spread(r, carry):
        a = x_ref[0, r].astype(F32)
        b = x_ref[1, r].astype(F32)
        mix = jnp.concatenate([a[:, LO:], b[:, LO:]], axis=1)
        for plane, v in enumerate((a[:, :LO], b[:, :LO], mix)):
            pd[pl.ds(pl.multiple_of(at(plane, 3 + r, 8), 8), COLS), :] = v
            xb[plane, r] = v.astype(BF16)
        return carry

    lax.fori_loop(0, ROWS, spread, 0)

    def pack(field, send, planes):
        for plane in range(planes):
            for k in range(3):
                send[0, plane, k] = field[pl.ds(at(plane, 3, 8 + k), ROWS, stride=WIDE), :].astype(BF16)
                send[1, plane, k] = field[pl.ds(at(plane, 3, 69 + k), ROWS, stride=WIDE), :].astype(BF16)

    pack(pd, sx, 3)

    peers = 21 + jnp.where(lat > 0, 3, 0) + jnp.where(lat < 3, 3, 0)
    peers = peers + jnp.where(top, 13 - jnp.where(zz >= 2, 1, 0), 0)
    pl.semaphore_wait(barrier, peers)

    def lat_copies(base, block, got):
        return (
            (lat < 3, remote(block.at[:, 13:16], got.at[0], base + LAT_AT, (lon, lat + 1))),
            (lat > 0, remote(block.at[:, 0:3], got.at[1], base + LAT_AT + 1, (lon, lat - 1))),
        )

    def lon_copies(base, send, got):
        found = []
        for side in range(2):
            for slot in range(3):
                dl = 1 - slot
                found.append((
                    (lat + dl >= 0) & (lat + dl <= 3),
                    remote(
                        send.at[1 - side], got.at[side, slot], base + LON_AT + 3 * side + slot,
                        (lon_of(1 - 2 * side), lat + dl),
                    ),
                ))
        return found

    def lon_arrives(slot):
        return (lat + slot - 1 >= 0) & (lat + slot - 1 <= 3)

    def fold1_copies(base, block, planes, got):
        found = []
        for k in range(6):
            width = 16 if k == 5 else COLS
            found.append((k != own1, remote(
                block.at[planes, 13:16, 0:width], got.at[k, :, :, 0:width], base + k,
                (fold1_to(k), lat),
            )))
        return found

    def fold2_copies(base, window, got):
        return [
            (k != own2, remote(window, got.at[k], base + ROUND + k, (fold2_peer(k), lat)))
            for k in range(8)
        ]

    def start_fold(base, block, planes, f1):
        for cond, copy in fold1_copies(base, block, planes, f1):
            pl.when(cond)(copy.start)

    def start_halo(base, block, send, rl, rc):
        for cond, copy in lon_copies(base, send, rc):
            pl.when(cond)(copy.start)
        for cond, copy in lat_copies(base, block, rl):
            pl.when(cond)(copy.start)

    def finish_halo(base, field, planes, block, send, rl, rc):
        lats = lat_copies(base, block, rl)
        for way, (arrives, row) in enumerate(((lat > 0, 0), (lat < 3, 19))):
            @pl.when(arrives)
            def _(way=way, row=row):
                lats[way][1].wait_recv()
                for plane in range(planes):
                    for r in range(3):
                        field[pl.ds(at(plane, row + r, 8), COLS), :] = rl[way, plane, r].astype(F32)
        lons = lon_copies(base, send, rc)
        for side in range(2):
            col = 5 if side == 0 else 72
            for slot in range(3):
                @pl.when(lon_arrives(slot))
                def _(side=side, slot=slot, col=col):
                    lons[3 * side + slot][1].wait_recv()
                    for plane in range(planes):
                        for k in range(3):
                            v = rc[side, slot, plane, k].astype(F32)
                            if slot == 1:
                                field[pl.ds(at(plane, 3, col + k), ROWS, stride=WIDE), :] = v
                            else:
                                for r in range(3):
                                    row = r if slot == 0 else 19 + r
                                    own = 13 + r if slot == 0 else r
                                    field[pl.ds(at(plane, row, col + k), 1), :] = v[own:own + 1]

    def shift_parts():
        begin = lax.rem(partner_ref[0] + (NLON - 2), NLON)
        return lax.rem(begin, COLS), lax.rem(lax.div(begin, COLS), 4), lax.div(begin, 4 * COLS)

    def make_window(base, block, planes, f1, window):
        offset, near, _ = shift_parts()
        for cond, copy in fold1_copies(base, block, planes, f1):
            pl.when(cond)(copy.wait_recv)

        @pl.when(zz >= 2)
        def _():
            f1[own1] = block[planes, 13:16]

        slot_at = lax.broadcasted_iota(jnp.int32, (WIDE, 3 * COLS), 0)
        from_at = lax.broadcasted_iota(jnp.int32, (WIDE, 3 * COLS), 1)
        pick = jnp.where(from_at + slot_at == offset + 74, 1.0, 0.0).astype(BF16)
        for plane in range(window.shape[0]):
            for r in range(3):
                three = jnp.concatenate([f1[near + c, plane, r] for c in range(3)], axis=0)
                window[plane, r] = dot(pick, three).astype(BF16)

    def middle_fold(base, block, planes, f1, window, f2):
        make_window(base, block, planes, f1, window)
        for cond, copy in fold2_copies(base, window, f2):
            pl.when(cond)(copy.start)
        f2[own2] = window[...]

    def foldy_copy(base, window, fy):
        return remote(window, fy.at[yh], base + ROUND, (xx * 8 + (1 - yh) * 4 + zz, lat))

    def foldy_from(base, window, fy):
        return remote(window, fy.at[1 - yh], base + ROUND, (xx * 8 + (1 - yh) * 4 + zz, lat))

    def foldx_copies(base, fy, fx):
        return [
            remote(fy.at[2], fx.at[xx], base + ROUND + k, (((xx + k) % 4) * 8 + yh * 4 + zz, lat))
            for k in (1, 2, 3)
        ]

    def foldx_from(base, fy, fx):
        return [
            remote(fy.at[2], fx.at[(xx + 4 - k) % 4], base + ROUND + k, (((xx + k) % 4) * 8 + yh * 4 + zz, lat))
            for k in (1, 2, 3)
        ]

    def fold_to_y(base, block, planes, f1, window, fy):
        make_window(base, block, planes, f1, window)
        foldy_copy(base, window, fy).start()
        fy[yh] = window[...]

    def fold_to_x(base, window, fy, fx):
        foldy_from(base, window, fy).wait_recv()
        far = shift_parts()[2]
        chosen = fy[lax.rem(1 - yh + far, 2)]
        fy[2] = chosen
        for copy in foldx_copies(base, fy, fx):
            copy.start()
        fx[xx] = chosen

    def end_fold(base, field, first, fy, fx):
        for copy in foldx_from(base, fy, fx):
            copy.wait_recv()
        far = shift_parts()[2]
        source = lax.div(lax.rem(7 - block8 + far, 8), 2)
        for plane in range(fx.shape[1]):
            for k in range(3):
                field[pl.ds(at(first + plane, 19 + k, 0), WIDE), :] = fx[source, plane, 2 - k].astype(F32)

    def close_three(base, block, planes, f1, window, fy, fx):
        for cond, copy in fold1_copies(base, block, planes, f1):
            pl.when(cond)(copy.wait_send)
        foldy_copy(base, window, fy).wait_send()
        for copy in foldx_copies(base, fy, fx):
            copy.wait_send()

    def finish_fold(base, field, first, window, f2):
        for cond, copy in fold2_copies(base, window, f2):
            pl.when(cond)(copy.wait_recv)
        far = shift_parts()[2]
        for plane in range(window.shape[0]):
            for k in range(3):
                field[pl.ds(at(first + plane, 19 + k, 0), WIDE), :] = f2[far, plane, 2 - k].astype(F32)

    def close_fold(base, block, planes, f1, window, f2):
        for cond, copy in fold1_copies(base, block, planes, f1):
            pl.when(cond)(copy.wait_send)
        for cond, copy in fold2_copies(base, window, f2):
            pl.when(cond)(copy.wait_send)

    def close_field(base, block, send, rl, rc):
        for cond, copy in lat_copies(base, block, rl):
            pl.when(cond)(copy.wait_send)
        for cond, copy in lon_copies(base, send, rc):
            pl.when(cond)(copy.wait_send)

    in_b, in_a, in_z = slice(1, 3), slice(0, 1), slice(0, 2)

    @pl.when(top)
    def _():
        start_fold(FOLD_B, xb, in_b, fb1)

    start_halo(0, xb, sx, rlx, rcx)

    for load in loads[1:]:
        load.wait()

    def clear_south(field, planes):
        for plane in range(planes):
            field[pl.ds(at(plane, 0, 0), 3 * WIDE), :] = jnp.zeros((3 * WIDE, LO), F32)

    clear_south(pd, 3)
    clear_south(pz, 2)

    lane = lax.broadcasted_iota(jnp.int32, (1, LO), 1)
    upper = lane >= 64

    def table(a, carry):
        low, high = dw_ref[a][:, :LO], dw_ref[a][:, LO:]
        mix = jnp.concatenate([high, high], axis=1)
        rlow, rhigh = dw_ref[6 - a][:, :LO], dw_ref[6 - a][:, LO:]
        rmix = jnp.concatenate([rhigh, rhigh], axis=1)
        for b in range(7):
            for kind, (v, w) in enumerate(((low, rlow), (mix, rmix))):
                straight = jnp.broadcast_to(v[b:b + 1], (8, LO))
                turned = jnp.broadcast_to(w[6 - b:7 - b], (8, LO))
                kt[kind, a * 7 + b] = straight
                kt[2 + kind, a * 7 + b] = turned
                kt[4 + kind, a * 7 + b] = jnp.where(top, straight, turned)
        return carry

    lax.fori_loop(0, 7, table, 0)
    wa[0:192] = win_ref[...]
    wa[192:256] = jnp.zeros((64, HID), BF16)
    wb[0:128] = win_ref[0:128]
    wb[128:192] = jnp.zeros((64, HID), BF16)
    wb[192:256] = win_ref[128:192]
    eye = jnp.where(
        lax.broadcasted_iota(jnp.int32, (COLS, COLS), 0) == lax.broadcasted_iota(jnp.int32, (COLS, COLS), 1),
        1.0, 0.0,
    ).astype(BF16)
    mask_t = dot(eye, mask_ref[...].astype(F32).astype(BF16), ((1,), (1,))).astype(BF16)
    for r in range(ROWS):
        one = jnp.where(lax.broadcasted_iota(jnp.int32, (ROWS, LO), 0) == r, 1.0, 0.0).astype(BF16)
        mb[r * COLS:(r + 1) * COLS] = dot(mask_t, one)
    gw[...] = jnp.zeros_like(gw)
    gwo[...] = jnp.zeros_like(gwo)
    gka[...] = jnp.zeros_like(gka)
    flat[KER_AT:2560] = jnp.zeros((2560 - KER_AT, LO), F32)
    for f1 in (fb1, fa1, fz1):
        f1[5, :, :, 16:64] = jnp.zeros_like(f1[5, :, :, 16:64])


    zero64 = jnp.zeros((1, 64), F32)

    def halves(ref, state):
        v = ref[...]
        high = v[:, LO:]
        parts = [high, zero64] if state == 0 else [zero64, high]
        return v[:, :LO], jnp.concatenate(parts, axis=1)

    def conv(field, plane, c, half, tab, tab_last):
        base = at(plane, 4 * c, 32 * half + 5)
        acc = [[jnp.zeros((8, LO), F32) for _ in range(4)] for _ in range(4)]
        for p in range(10):
            for b in range(7):
                use = tab_last if p >= 7 else tab
                ks = {r: kt[use, (p - r) * 7 + b] for r in range(4) if 0 <= p - r <= 6}
                for t in range(4):
                    v = field[pl.ds(base + p * WIDE + 8 * t + b, 8), :]
                    for r, kv in ks.items():
                        acc[r][t] = acc[r][t] + kv * v
        return acc

    def bias(s):
        return jnp.concatenate([bin_ref[2 * s:2 * s + 1], bin_ref[2 * s + 1:2 * s + 2]], axis=1)

    def norm(c, state):
        here = pl.ds(pl.multiple_of(c * CHUNK, CHUNK), CHUNK)
        keep = upper if state == 1 else jnp.logical_not(upper)
        blo, bhi = halves(dwb_ref, state)
        glo, ghi = halves(g_ref, state)
        llo, lhi = halves(lb_ref, state)
        lo = dp[state, here] + blo
        hi = jnp.where(keep, dp[2, here] + bhi, 0.0)
        mean = jnp.sum(lo + hi, axis=1, keepdims=True) * (1.0 / CH)
        lo = lo - mean
        hi = jnp.where(keep, hi - mean, 0.0)
        inv = lax.rsqrt(jnp.sum(lo * lo + hi * hi, axis=1, keepdims=True) * (1.0 / CH) + norm_eps)
        nlo, nhi = lo * inv, hi * inv
        low = jnp.concatenate(
            [(nlo * glo + llo).astype(BF16), (nhi * ghi + lhi).astype(BF16)], axis=1
        )
        return low, nlo, nhi, inv, glo, ghi, keep

    def forward_chunk(c):
        low = norm(c, 0)[0]
        mixed = jnp.broadcast_to(bout_ref[...], (CHUNK, CH))
        for s in range(3):
            cut = slice(256 * s, 256 * s + 256)
            u = dot(low, wa[:, cut]) + bias(s)
            t = jnp.tanh(u * (root_factor + (root_factor * cubic_coef) * (u * u)))
            act = (u * (0.5 + 0.5 * t)).astype(BF16)
            mixed = mixed + dot(act, wout_ref[:, cut], ((1,), (1,)))
        mixed = mixed * ls_ref[...]
        here = pl.ds(pl.multiple_of(c * CHUNK, CHUNK), CHUNK)
        m = mb[here]
        mm = jnp.concatenate([m, m[:, :64]], axis=1)
        for r in range(4):
            cut = slice(64 * r, 64 * r + 64)
            outa_ref[4 * c + r] = (x_ref[0, 4 * c + r].astype(F32) + mm[cut] * mixed[cut]).astype(BF16)

    def backward_chunk(c):
        low, nlo, nhi, inv, glo, ghi, keep = norm(c, 1)
        here = pl.ds(pl.multiple_of(c * CHUNK, CHUNK), CHUNK)
        m = mb[here]
        mm = jnp.concatenate([m, m[:, :64]], axis=1)
        go = jnp.concatenate([go_ref[4 * c + r] for r in range(4)], axis=0).astype(F32)
        gl = (mm * (ls_ref[...] * go)).astype(BF16)
        gn = jnp.zeros((CHUNK, 256), F32)
        for s in range(3):
            cut = slice(256 * s, 256 * s + 256)
            u = dot(low, wb[:, cut]) + bias(s)
            u2 = u * u
            t = jnp.tanh(u * (root_factor + (root_factor * cubic_coef) * u2))
            half = 0.5 + 0.5 * t
            value = u * half
            slope = half + value * (1.0 - t) * (root_factor + (3.0 * root_factor * cubic_coef) * u2)
            act = value.astype(BF16)
            gwo[:, cut] += dot(gl, act, ((0,), (0,)))
            gh = (dot(gl, wout_ref[:, cut]) * slope).astype(BF16)
            gw[:, cut] += dot(low, gh, ((0,), (0,)))
            gn = gn + dot(gh, wb[:, cut], ((1,), (1,)))
        nl, nh = gn[:, :LO] * glo, gn[:, LO:] * ghi
        one = jnp.sum(nl + nh, axis=1, keepdims=True) * (1.0 / CH)
        two = jnp.sum(nl * nlo + nh * nhi, axis=1, keepdims=True) * (1.0 / CH)
        zl = inv * (nl - one - nlo * two)
        zh = jnp.where(keep, inv * (nh - one - nhi * two), 0.0)
        for plane, v in enumerate((zl, zh)):
            for r in range(4):
                cut = slice(64 * r, 64 * r + 64)
                pz[pl.ds(pl.multiple_of(at(plane, 3 + 4 * c + r, 8), 8), COLS), :] = v[cut]
                zb[plane, 4 * c + r] = v[cut].astype(BF16)

    def sweep_states(plane, c):
        def sweep(half, carry):
            kind = plane // 2
            acc = conv(pd, plane, c, half, kind, kind)
            for r in range(4):
                for t in range(4):
                    cell = pl.multiple_of(c * CHUNK + r * COLS + half * 32 + 8 * t, 8)
                    dp[plane, pl.ds(cell, 8)] = acc[r][t]
            return carry

        lax.fori_loop(0, 2, sweep, 0)

    def kernel_chunk(c):
        for plane in range(2):
            for rows in ((0, 1, 2, 3), (4, 5, 6)):
                def add_row(i, acc, plane=plane, rows=rows):
                    acc = list(acc)
                    for t in range(8):
                        z = pz[pl.ds(pl.multiple_of(at(plane, 3 + i, 8 + 8 * t), 8), 8), :]
                        for n, a in enumerate(rows):
                            for b in range(7):
                                v = pd[pl.ds(at(1 + plane, i + a, 5 + 8 * t + b), 8), :]
                                acc[n * 7 + b] = acc[n * 7 + b] + v * z
                    return tuple(acc)

                acc = lax.fori_loop(
                    4 * c, 4 * c + 4, add_row,
                    tuple(jnp.zeros((8, LO), F32) for _ in range(7 * len(rows))),
                )
                for n, a in enumerate(rows):
                    for b in range(7):
                        gka[plane, a * 7 + b] += acc[n * 7 + b]

    finish_halo(0, pd, 3, xb, sx, rlx, rcx)

    def first_pass(c, carry):
        @pl.when(top & (c == 2))
        def _():
            fold_to_y(FOLD_A, xb, in_a, fa1, va, fya)

        @pl.when(top & (c == 3))
        def _():
            finish_fold(FOLD_B, pd, 1, vb, fb2)
            fold_to_x(FOLD_A, va, fya, fxa)

        def both(plane, carry):
            sweep_states(plane, c)
            return carry

        lax.fori_loop(1, 3, both, 0)

        @pl.when(top & (c == 0))
        def _():
            middle_fold(FOLD_B, xb, in_b, fb1, vb, fb2)
            start_fold(FOLD_A, xb, in_a, fa1)

        backward_chunk(c)
        kernel_chunk(c)
        return carry

    lax.fori_loop(0, 4, first_pass, 0)

    for plane in range(2):
        for n in range(49):
            line = KER_AT + plane * 56 + n
            flat[line:line + 1] = jnp.sum(gka[plane, n], axis=0, keepdims=True)

    for s in range(6):
        cut = slice(128 * s, 128 * s + 128)
        flat[WIN_AT + 192 * s:WIN_AT + 192 * s + 128] = gw[0:128, cut]
        flat[WIN_AT + 192 * s + 128:WIN_AT + 192 * s + 192] = gw[192:256, cut]
        flat[WOUT_AT + 192 * s:WOUT_AT + 192 * s + 192] = gwo[:, cut]

    def half_at(which):
        return pl.ds(pl.multiple_of(which * HALF, 8), HALF)

    b0[...] = flat[half_at(1 - core)].astype(BF16)
    s0 = remote(b0, r0, S0_AT, mate)

    def s1(m):
        return remote(hb.at[place_of(m)], r1.at[m - 1], S1_AT + m - 1, plane_peer(m))

    def s3(k):
        return remote(r3.at[yy], r3.at[yy], S3_AT + k - 1, third_peer(k))

    def s3_from(k):
        return remote(r3.at[yy], r3.at[(yy + 4 - k) % 4], S3_AT + k - 1, third_peer(k))

    def g1(m):
        return remote(ag.at[core, place], ag.at[core, place], G1_AT + m - 1, plane_peer(m))

    def g1_from(m):
        there = ((xx + 4 - m // 4) % 4) * 4 + (zz + 4 - m % 4) % 4
        return remote(ag.at[core, place], ag.at[core, there], G1_AT + m - 1, plane_peer(m))

    g3 = remote(ag.at[core], ag.at[core], G3_AT, mate)
    g3_from = remote(ag.at[core], ag.at[1 - core], G3_AT, mate)

    s0.start()

    pack(pz, sz, 2)

    @pl.when(top)
    def _():
        start_fold(FOLD_Z, zb, in_z, fz1)

    start_halo(FIELD, zb, sz, rlz, rcz)

    def second_pass(c, carry):
        @pl.when(c == 1)
        def _():
            s0.wait_recv()
            for i in range(16):
                part = pl.ds(pl.multiple_of(core * HALF + i * PIECE, 8), PIECE)
                total = flat[part] + r0[i * PIECE:(i + 1) * PIECE].astype(F32)
                flat[part] = total
                hb[i] = total.astype(BF16)
            for m in range(1, 16):
                s1(m).start()

        @pl.when(top & (c == 3))
        def _():
            end_fold(FOLD_A, pd, 0, fya, fxa)

        sweep_states(0, c)
        forward_chunk(c)
        return carry

    lax.fori_loop(0, 4, second_pass, 0)

    finish_halo(FIELD, pz, 2, zb, sz, rlz, rcz)

    @pl.when(top)
    def _():
        fold_to_y(FOLD_Z, zb, in_z, fz1, vz, fyz)

    def third_pass(c, carry):
        @pl.when(c == 1)
        def _():
            for m in range(1, 16):
                s1(m).wait_recv()
            total = flat[pl.ds(pl.multiple_of(core * HALF + place * PIECE, 8), PIECE)]
            for m in range(15):
                total = total + r1[m].astype(F32)
            r3[yy] = total
            for k in (1, 2, 3):
                s3(k).start()

        @pl.when(top & (c == 2))
        def _():
            fold_to_x(FOLD_Z, vz, fyz, fxz)

        @pl.when(c == 3)
        def _():
            for k in (1, 2, 3):
                s3_from(k).wait_recv()
            ag[core, place] = ((r3[0] + r3[1] + r3[2] + r3[3]) * scale).astype(BF16)
            for m in range(1, 16):
                g1(m).start()

        @pl.when(top & (c == 3))
        def _():
            end_fold(FOLD_Z, pz, 0, fyz, fxz)

        last = jnp.where(c == 3, 4, 2)

        def sweep(half, carry):
            at_col = pl.ds(pl.multiple_of(32 * half, 32), 32)
            acc_lo = conv(pz, 0, c, half, 2, last)
            for r in range(4):
                low = jnp.concatenate(acc_lo[r], axis=0)
                go = go_ref[4 * c + r, at_col, :].astype(F32)
                gs_ref[4 * c + r, at_col, 0:LO] = low + go[:, :LO]
            acc_hi = conv(pz, 1, c, half, 3, last + 1)
            for r in range(4):
                high = jnp.concatenate(acc_hi[r], axis=0)
                go = go_ref[4 * c + r, at_col, :].astype(F32)
                gs_ref[4 * c + r, at_col, LO:CH] = high[:, 64:] + go[:, LO:]
            return carry

        lax.fori_loop(0, 2, sweep, 0)
        return carry

    lax.fori_loop(0, 4, third_pass, 0)

    for m in range(1, 16):
        g1_from(m).wait_recv()
    g3.start()
    g3_from.wait_recv()

    def part_of(start, size):
        first, end = start // PIECE, -(-(start + size) // PIECE)
        found = [ag[i // 16, i % 16] for i in range(first, end)]
        return jnp.concatenate(found, axis=0)[start - first * PIECE:start - first * PIECE + size].astype(F32)

    for s in range(6):
        gwin_ref[:, 128 * s:128 * s + 128] = part_of(WIN_AT + 192 * s, 192)
        gwout_ref[:, 128 * s:128 * s + 128] = part_of(WOUT_AT + 192 * s, 192)
    klow = part_of(KER_AT, 56)
    khigh = part_of(KER_AT + 56, 56)
    for a in range(7):
        gk_ref[a, :, 0:LO] = klow[7 * a:7 * a + 7]
        gk_ref[a, :, LO:CH] = khigh[7 * a:7 * a + 7, 64:]

    close_field(0, xb, sx, rlx, rcx)
    close_field(FIELD, zb, sz, rlz, rcz)

    @pl.when(top)
    def _():
        close_fold(FOLD_B, xb, in_b, fb1, vb, fb2)
        close_three(FOLD_A, xb, in_a, fa1, va, fya, fxa)
        close_three(FOLD_Z, zb, in_z, fz1, vz, fyz, fxz)

    s0.wait_send()
    for m in range(1, 16):
        s1(m).wait_send()
        g1(m).wait_send()
    for k in (1, 2, 3):
        s3(k).wait_send()
    g3.wait_send()


def move(*refs):
    count = (len(refs) - 2) // 3
    ins, outs, held = refs[:count], refs[count:2 * count], refs[2 * count:3 * count]
    come, go = refs[-2:]
    first = [pltpu.make_async_copy(ins[i], held[i], come.at[i]) for i in range(count)]
    second = [pltpu.make_async_copy(held[i], outs[i], go.at[i]) for i in range(count)]
    for copy in first:
        copy.start()
    for i in range(count):
        first[i].wait()
        second[i].start()
    for copy in second:
        copy.wait()


def shards(states, grad_out, land_mask, partner, dw_kernel, dw_bias, ln_gain, ln_bias, w_in, b_in,
           w_out, b_out, layer_scale):
    def row(v):
        return v.reshape(1, v.shape[0])

    vmem = pl.BlockSpec(memory_space=pltpu.VMEM)
    anywhere = pl.BlockSpec(memory_space=pl.ANY)

    def buf(*shape, dtype=F32):
        return pltpu.VMEM(shape, dtype)

    load_to = [
        buf(2, ROWS, COLS, CH, dtype=BF16), buf(ROWS, COLS, CH, dtype=BF16),
        buf(ROWS, COLS, dtype=jnp.int32), pltpu.SMEM((NLON,), jnp.int32), buf(7, 7, CH),
        buf(1, CH), buf(1, CH), buf(1, CH), buf(CH, HID, dtype=BF16), buf(HID // LO, LO),
        buf(CH, HID, dtype=BF16), buf(1, CH), buf(1, CH), pltpu.SemaphoreType.DMA((13,)),
    ]
    scratch = load_to + [
        buf(3 * PROWS * WIDE, LO), buf(2 * PROWS * WIDE, LO),
        buf(3, ROWS, COLS, LO, dtype=BF16), buf(2, ROWS, COLS, LO, dtype=BF16),
        buf(2, 3, 3, ROWS, LO, dtype=BF16), buf(2, 2, 3, ROWS, LO, dtype=BF16),
        buf(2, 3, 3, COLS, LO, dtype=BF16), buf(2, 2, 3, COLS, LO, dtype=BF16),
        buf(2, 3, 3, 3, ROWS, LO, dtype=BF16), buf(2, 3, 2, 3, ROWS, LO, dtype=BF16),
        buf(6, 2, 3, COLS, LO, dtype=BF16), buf(6, 1, 3, COLS, LO, dtype=BF16),
        buf(6, 2, 3, COLS, LO, dtype=BF16),
        buf(2, 3, WIDE, LO, dtype=BF16), buf(1, 3, WIDE, LO, dtype=BF16), buf(2, 3, WIDE, LO, dtype=BF16),
        buf(8, 2, 3, WIDE, LO, dtype=BF16),
        buf(3, 1, 3, WIDE, LO, dtype=BF16), buf(3, 2, 3, WIDE, LO, dtype=BF16),
        buf(4, 1, 3, WIDE, LO, dtype=BF16), buf(4, 2, 3, WIDE, LO, dtype=BF16),
        buf(3, CELLS, LO), buf(CELLS, LO), buf(6, 49, 8, LO),
        buf(256, HID, dtype=BF16), buf(256, HID, dtype=BF16),
        buf(256, HID), buf(CH, HID), buf(2, 49, 8, LO), buf(2 * HALF, LO),
        buf(HALF, LO, dtype=BF16), buf(HALF, LO, dtype=BF16),
        buf(16, PIECE, LO, dtype=BF16), buf(15, PIECE, LO, dtype=BF16), buf(4, PIECE, LO),
        buf(2, 16, PIECE, LO, dtype=BF16),
        pltpu.SemaphoreType.DMA((COPIES,)), pltpu.SemaphoreType.DMA((COPIES,)),
    ]
    outs = (
        jax.ShapeDtypeStruct((ROWS, COLS, CH), BF16),
        jax.ShapeDtypeStruct((ROWS, COLS, CH), F32),
        jax.ShapeDtypeStruct((7, 7, CH), F32),
        jax.ShapeDtypeStruct((CH, HID), F32),
        jax.ShapeDtypeStruct((CH, HID), F32),
    )
    found = pl.pallas_call(
        kernel,
        out_shape=outs,
        in_specs=[anywhere] * 13,
        out_specs=(vmem,) * 5,
        scratch_shapes=scratch,
        compiler_params=pltpu.CompilerParams(
            collective_id=0, has_side_effects=True, vmem_limit_bytes=60 * 1024 * 1024
        ),
        name="block",
    )(
        states, grad_out, land_mask, partner, dw_kernel, row(dw_bias), row(ln_gain), row(ln_bias),
        w_in, b_in.reshape(HID // LO, LO), w_out.T, row(b_out), row(layer_scale),
    )
    out_a, grad_states, grad_kernel, grad_win, grad_wout = pl.pallas_call(
        move,
        out_shape=outs,
        in_specs=[anywhere] * 5,
        out_specs=(anywhere,) * 5,
        scratch_shapes=[pltpu.VMEM(o.shape, o.dtype) for o in outs]
        + [pltpu.SemaphoreType.DMA((5,)), pltpu.SemaphoreType.DMA((5,))],
        name="move",
    )(*found)
    return out_a, grad_states, grad_kernel, grad_win, grad_wout.T


def solution(mesh):
    placed = (
        P(None, "lat", "lon", None), P("lat", "lon", None), P("lat", "lon"),
        P(), P(), P(), P(), P(), P(), P(), P(), P(), P(),
    )
    return jax.shard_map(
        shards,
        mesh=mesh,
        in_specs=placed,
        out_specs=(P("lat", "lon", None), P("lat", "lon", None), P(), P(), P()),
        check_vma=False,
    )
```

time: 94.2 us -> 71.7 us (0.76)
  Pallas kernels: 83.5 us -> 70.9 us
  local copies, waits for them, and re-layouts: 9.72 us -> 0 us
    pallas_call x1 -> x2, Pallas kernels: 83.5 us -> 70.9 us  [the longest x1 68 us: shards(): pl.pallas_call(kernel, out_shape=outs, in_specs=[anywhere] * 13, out_spec...]
    unnamed x13 -> x0, local copies, waits for them, and re-layouts: 6.86 us -> none
    pallas_call x1 -> x0, local copies, waits for them, and re-layouts: 2.29 us -> none  [shards(): pl.pallas_call(kernel, out_shape=outs, in_specs=[vmem, vmem, vmem, smem]...]
where the time goes in v2:
time: 71.7 us; the launch traced here: 71.5 us
  Pallas kernels  70.9 us (99%)
    pallas_call x1, Pallas kernels, shards(): pl.pallas_call(kernel, out_shape=outs, in_specs=[anywhere] * 13, out_spec...  68 us
    pallas_call x1, Pallas kernels, shards(): pl.pallas_call(move, out_shape=outs, in_specs=[anywhere] * 5, out_specs=(...  2.85 us

profile of v2, /device:TPU:1, one launch (start us, length us, event | category | flops | bytes accessed | tf_op | source)
XLA Modules:
  0.0 71.5 jit_solution(7972779356236830034)
XLA Ops:
  0.6 68.0 %block.1 = (bf16[16,64,192]{2,1,0:T(8,128)(2,1)}, f32[16,64,192]{2,1,0:T(8,128)}, f32[7,7,192]{2,1,0:T(8,128)}, f32[192,768]{1,0:T(8,128)}, f32[192,768]{1,0:T(8,128)}) custom-call(bf16[2,16,64,192]{3,2,1,0:T(8,128)(2,1)} %x_in.1, bf16[16,64,192]{2,1,0:T(8,128)(2,1)} %go_in.1, s32[16,64]{1,0:T(8,128)} %mask_in.1, s32[2048]{0:T(1024)} %partner_in.1, ...), custom_call_target="tpu_custom_call" | custom-call | tf_op jit(solution)/shard_map/block/pallas_call | solution.py:767
  68.7 2.8 %move.1 = (bf16[16,64,192]{2,1,0:T(8,128)(2,1)}, f32[16,64,192]{2,1,0:T(8,128)}, f32[7,7,192]{2,1,0:T(8,128)}, f32[192,768]{1,0:T(8,128)}, f32[192,768]{1,0:T(8,128)}) custom-call(bf16[16,64,192]{2,1,0:T(8,128)(2,1)} %get-tuple-element.15.refs_0_, f32[16,64,192]{2,1,0:T(8,128)} %get-tuple-element.16.refs_1_, f32[7,7,192]{2,1,0:T(8,128)} %get-tuple-element.17.refs_2_, ...), custom_call_target="tpu_custom_call" | custom-call | tf_op jit(solution)/shard_map/move/pallas_call | solution.py:781

commit v3 on v2

--- a/solution.py
+++ b/solution.py
@@ -25,7 +25,7 @@
 PIECE = 80
 HALF = 16 * PIECE
 QUART = 4 * PIECE
-WIN_AT, WOUT_AT, KER_AT = 0, 1152, 2304
+WIN_AT, WOUT_AT, REST_AT = 0, 1152, 2304
 
 root_factor = math.sqrt(2.0 / math.pi)
 cubic_coef = 0.044715
@@ -35,7 +35,8 @@
 LAT_AT, LON_AT, FIELD = 0, 2, 8
 FOLD_B, FOLD_A, FOLD_Z, ROUND = 16, 30, 44, 6
 S0_AT, S1_AT, S3_AT, G1_AT, G3_AT = 58, 59, 74, 77, 92
-COPIES = 93
+K0_AT, K1_AT, K3_AT, K4_AT = 96, 97, 112, 115
+COPIES = 130
 
 
 def dot(a, b, dims=((1,), (0,))):
@@ -45,9 +46,9 @@
 def kernel(
     x_in, go_in, mask_in, partner_in, dw_in, dwb_in, g_in, lb_in, win_in, bin_in,
     wout_in, bout_in, ls_in,
-    outa_ref, gs_ref, gk_ref, gwin_ref, gwout_ref,
+    outa_out, gs_out, gk_ref, ag_out,
     x_ref, go_ref, mask_ref, partner_ref, dw_ref, dwb_ref, g_ref, lb_ref, win_ref, bin_ref,
-    wout_ref, bout_ref, ls_ref, load_sem,
+    wout_ref, bout_ref, ls_ref, load_sem, outa_ref, gs_ref, store_sem, gkf, kr0, ksum, kr1, kr3, kag,
     pd, pz, xb, zb, sx, sz, rlx, rlz, rcx, rcz, fb1, fa1, fz1, vb, va, vz, fb2, fya, fyz, fxa, fxz,
     dp, mb, kt, wa, wb, gw, gwo, gka, flat, b0, r0, hb, r1, r3, ag, ssem, rsem,
 ):
@@ -387,7 +388,8 @@
     gw[...] = jnp.zeros_like(gw)
     gwo[...] = jnp.zeros_like(gwo)
     gka[...] = jnp.zeros_like(gka)
-    flat[KER_AT:2560] = jnp.zeros((2560 - KER_AT, LO), F32)
+    flat[REST_AT:2560] = jnp.zeros((2560 - REST_AT, LO), F32)
+    gkf[112:128] = jnp.zeros((16, LO), F32)
     for f1 in (fb1, fa1, fz1):
         f1[5, :, :, 16:64] = jnp.zeros_like(f1[5, :, :, 16:64])
 
@@ -516,17 +518,18 @@
                     for b in range(7):
                         gka[plane, a * 7 + b] += acc[n * 7 + b]
 
+    @pl.when(top)
+    def _():
+        middle_fold(FOLD_B, xb, in_b, fb1, vb, fb2)
+        start_fold(FOLD_A, xb, in_a, fa1)
+
     finish_halo(0, pd, 3, xb, sx, rlx, rcx)
 
     def first_pass(c, carry):
-        @pl.when(top & (c == 2))
-        def _():
+        @pl.when(top & (c == 3))
+        def _():
+            finish_fold(FOLD_B, pd, 1, vb, fb2)
             fold_to_y(FOLD_A, xb, in_a, fa1, va, fya)
-
-        @pl.when(top & (c == 3))
-        def _():
-            finish_fold(FOLD_B, pd, 1, vb, fb2)
-            fold_to_x(FOLD_A, va, fya, fxa)
 
         def both(plane, carry):
             sweep_states(plane, c)
@@ -534,21 +537,10 @@
 
         lax.fori_loop(1, 3, both, 0)
 
-        @pl.when(top & (c == 0))
-        def _():
-            middle_fold(FOLD_B, xb, in_b, fb1, vb, fb2)
-            start_fold(FOLD_A, xb, in_a, fa1)
-
         backward_chunk(c)
-        kernel_chunk(c)
         return carry
 
     lax.fori_loop(0, 4, first_pass, 0)
-
-    for plane in range(2):
-        for n in range(49):
-            line = KER_AT + plane * 56 + n
-            flat[line:line + 1] = jnp.sum(gka[plane, n], axis=0, keepdims=True)
 
     for s in range(6):
         cut = slice(128 * s, 128 * s + 128)
@@ -578,8 +570,31 @@
         there = ((xx + 4 - m // 4) % 4) * 4 + (zz + 4 - m % 4) % 4
         return remote(ag.at[core, place], ag.at[core, there], G1_AT + m - 1, plane_peer(m))
 
-    g3 = remote(ag.at[core], ag.at[core], G3_AT, mate)
-    g3_from = remote(ag.at[core], ag.at[1 - core], G3_AT, mate)
+    def g3(d):
+        rows = pl.ds(pl.multiple_of(((xx + 4 - d) % 4) * 4, 4), 4)
+        return remote(ag.at[core, rows], ag.at[core, rows], G3_AT + d, mate)
+
+    def g3_from(d):
+        rows = pl.ds(pl.multiple_of(((xx + 4 - d) % 4) * 4, 4), 4)
+        return remote(ag.at[core, rows], ag.at[1 - core, rows], G3_AT + d, mate)
+
+    k0 = remote(gkf, kr0, K0_AT, mate)
+
+    def k1(m):
+        return remote(ksum.at[place_of(m)], kr1.at[m - 1], K1_AT + m - 1, plane_peer(m))
+
+    def k3(k):
+        return remote(kr3.at[yy], kr3.at[yy], K3_AT + k - 1, third_peer(k))
+
+    def k3_from(k):
+        return remote(kr3.at[yy], kr3.at[(yy + 4 - k) % 4], K3_AT + k - 1, third_peer(k))
+
+    def k4(m):
+        return remote(kag.at[place], kag.at[place], K4_AT + m - 1, plane_peer(m))
+
+    def k4_from(m):
+        there = ((xx + 4 - m // 4) % 4) * 4 + (zz + 4 - m % 4) % 4
+        return remote(kag.at[place], kag.at[there], K4_AT + m - 1, plane_peer(m))
 
     s0.start()
 
@@ -592,7 +607,7 @@
     start_halo(FIELD, zb, sz, rlz, rcz)
 
     def second_pass(c, carry):
-        @pl.when(c == 1)
+        @pl.when(c == 2)
         def _():
             s0.wait_recv()
             for i in range(16):
@@ -603,21 +618,49 @@
             for m in range(1, 16):
                 s1(m).start()
 
-        @pl.when(top & (c == 3))
-        def _():
-            end_fold(FOLD_A, pd, 0, fya, fxa)
+        @pl.when(top & (c == 2))
+        def _():
+            fold_to_x(FOLD_A, va, fya, fxa)
+
+        kernel_chunk(c)
+        return carry
+
+    lax.fori_loop(0, 4, second_pass, 0)
+
+    for plane in range(2):
+        for n in range(49):
+            line = plane * 56 + n
+            gkf[line:line + 1] = jnp.sum(gka[plane, n], axis=0, keepdims=True)
+        gkf[plane * 56 + 49:plane * 56 + 56] = jnp.zeros((7, LO), F32)
+    k0.start()
+
+    def state_pass(c, carry):
+        @pl.when(c == 2)
+        def _():
+            k0.wait_recv()
+            for i in range(16):
+                ksum[i] = gkf[8 * i:8 * i + 8] + kr0[8 * i:8 * i + 8]
+            for m in range(1, 16):
+                k1(m).start()
 
         sweep_states(0, c)
         forward_chunk(c)
         return carry
 
-    lax.fori_loop(0, 4, second_pass, 0)
+    lax.fori_loop(0, 3, state_pass, 0)
 
     finish_halo(FIELD, pz, 2, zb, sz, rlz, rcz)
 
     @pl.when(top)
     def _():
         fold_to_y(FOLD_Z, zb, in_z, fz1, vz, fyz)
+
+    stores = [
+        pltpu.make_async_copy(outa_ref, outa_out, store_sem.at[0]),
+        pltpu.make_async_copy(gs_ref, gs_out, store_sem.at[1]),
+        pltpu.make_async_copy(ag.at[core], ag_out.at[core], store_sem.at[2]),
+        pltpu.make_async_copy(ag.at[1 - core], ag_out.at[1 - core], store_sem.at[3]),
+    ]
 
     def third_pass(c, carry):
         @pl.when(c == 1)
@@ -631,6 +674,17 @@
             for k in (1, 2, 3):
                 s3(k).start()
 
+        @pl.when(c == 2)
+        def _():
+            for m in range(1, 16):
+                k1(m).wait_recv()
+            total = ksum[place]
+            for m in range(15):
+                total = total + kr1[m]
+            kr3[yy] = total
+            for k in (1, 2, 3):
+                k3(k).start()
+
         @pl.when(top & (c == 2))
         def _():
             fold_to_x(FOLD_Z, vz, fyz, fxz)
@@ -642,6 +696,21 @@
             ag[core, place] = ((r3[0] + r3[1] + r3[2] + r3[3]) * scale).astype(BF16)
             for m in range(1, 16):
                 g1(m).start()
+
+        @pl.when(top & (c == 3))
+        def _():
+            end_fold(FOLD_A, pd, 0, fya, fxa)
+
+        @pl.when(c == 3)
+        def _():
+            sweep_states(0, 3)
+            forward_chunk(3)
+            stores[0].start()
+            for k in (1, 2, 3):
+                k3_from(k).wait_recv()
+            kag[place] = (kr3[0] + kr3[1] + kr3[2] + kr3[3]) * scale
+            for m in range(1, 16):
+                k4(m).start()
 
         @pl.when(top & (c == 3))
         def _():
@@ -668,24 +737,21 @@
 
     lax.fori_loop(0, 4, third_pass, 0)
 
+    stores[1].start()
+    for d in (0, 1, 3, 2):
+        for m in range(max(4 * d, 1), 4 * d + 4):
+            g1_from(m).wait_recv()
+        g3(d).start()
+    stores[2].start()
     for m in range(1, 16):
-        g1_from(m).wait_recv()
-    g3.start()
-    g3_from.wait_recv()
-
-    def part_of(start, size):
-        first, end = start // PIECE, -(-(start + size) // PIECE)
-        found = [ag[i // 16, i % 16] for i in range(first, end)]
-        return jnp.concatenate(found, axis=0)[start - first * PIECE:start - first * PIECE + size].astype(F32)
-
-    for s in range(6):
-        gwin_ref[:, 128 * s:128 * s + 128] = part_of(WIN_AT + 192 * s, 192)
-        gwout_ref[:, 128 * s:128 * s + 128] = part_of(WOUT_AT + 192 * s, 192)
-    klow = part_of(KER_AT, 56)
-    khigh = part_of(KER_AT + 56, 56)
+        k4_from(m).wait_recv()
+    kall = jnp.concatenate([kag[i] for i in range(14)], axis=0)
     for a in range(7):
-        gk_ref[a, :, 0:LO] = klow[7 * a:7 * a + 7]
-        gk_ref[a, :, LO:CH] = khigh[7 * a:7 * a + 7, 64:]
+        gk_ref[a, :, 0:LO] = kall[7 * a:7 * a + 7]
+        gk_ref[a, :, LO:CH] = kall[56 + 7 * a:56 + 7 * a + 7, 64:]
+    for d in range(4):
+        g3_from(d).wait_recv()
+    stores[3].start()
 
     close_field(0, xb, sx, rlx, rcx)
     close_field(FIELD, zb, sz, rlz, rcz)
@@ -702,20 +768,48 @@
         g1(m).wait_send()
     for k in (1, 2, 3):
         s3(k).wait_send()
-    g3.wait_send()
-
-
-def move(*refs):
-    count = (len(refs) - 2) // 3
-    ins, outs, held = refs[:count], refs[count:2 * count], refs[2 * count:3 * count]
-    come, go = refs[-2:]
-    first = [pltpu.make_async_copy(ins[i], held[i], come.at[i]) for i in range(count)]
-    second = [pltpu.make_async_copy(held[i], outs[i], go.at[i]) for i in range(count)]
+    for d in range(4):
+        g3(d).wait_send()
+    k0.wait_send()
+    for m in range(1, 16):
+        k1(m).wait_send()
+        k4(m).wait_send()
+    for k in (1, 2, 3):
+        k3(k).wait_send()
+    for store in stores:
+        store.wait()
+
+
+def part_of(ag, start, size):
+    first, end = start // PIECE, -(-(start + size) // PIECE)
+    found = [ag[i // 16, i % 16] for i in range(first, end)]
+    return jnp.concatenate(found, axis=0)[start - first * PIECE:start - first * PIECE + size].astype(F32)
+
+
+def finish(
+    outa_in, gs_in, gk_in, ag_in, outa_out, gs_out, gk_out, gwin_out, gwout_out,
+    outa, gs, gk, ag, gwin, gwout, come, go,
+):
+    first = [
+        pltpu.make_async_copy(a, b, come.at[i])
+        for i, (a, b) in enumerate(((ag_in, ag), (gs_in, gs), (outa_in, outa), (gk_in, gk)))
+    ]
+    second = [
+        pltpu.make_async_copy(a, b, go.at[i])
+        for i, (a, b) in enumerate(((gs, gs_out), (outa, outa_out), (gk, gk_out), (gwin, gwin_out), (gwout, gwout_out)))
+    ]
     for copy in first:
         copy.start()
-    for i in range(count):
-        first[i].wait()
+    first[0].wait()
+    for s in range(6):
+        gwin[:, 128 * s:128 * s + 128] = part_of(ag, WIN_AT + 192 * s, 192)
+    second[3].start()
+    for i in range(3):
+        first[i + 1].wait()
         second[i].start()
+    for s in range(6):
+        gwout[:, 128 * s:128 * s + 128] = part_of(ag, WOUT_AT + 192 * s, 192)
+    second[4].start()
     for copy in second:
         copy.wait()
 
@@ -736,6 +830,8 @@
         buf(ROWS, COLS, dtype=jnp.int32), pltpu.SMEM((NLON,), jnp.int32), buf(7, 7, CH),
         buf(1, CH), buf(1, CH), buf(1, CH), buf(CH, HID, dtype=BF16), buf(HID // LO, LO),
         buf(CH, HID, dtype=BF16), buf(1, CH), buf(1, CH), pltpu.SemaphoreType.DMA((13,)),
+        buf(ROWS, COLS, CH, dtype=BF16), buf(ROWS, COLS, CH), pltpu.SemaphoreType.DMA((4,)),
+        buf(128, LO), buf(128, LO), buf(16, 8, LO), buf(15, 8, LO), buf(4, 8, LO), buf(16, 8, LO),
     ]
     scratch = load_to + [
         buf(3 * PROWS * WIDE, LO), buf(2 * PROWS * WIDE, LO),
@@ -766,9 +862,9 @@
     )
     found = pl.pallas_call(
         kernel,
-        out_shape=outs,
+        out_shape=outs[:3] + (jax.ShapeDtypeStruct((2, 16, PIECE, LO), BF16),),
         in_specs=[anywhere] * 13,
-        out_specs=(vmem,) * 5,
+        out_specs=(anywhere, anywhere, vmem, anywhere),
         scratch_shapes=scratch,
         compiler_params=pltpu.CompilerParams(
             collective_id=0, has_side_effects=True, vmem_limit_bytes=60 * 1024 * 1024
@@ -779,13 +875,15 @@
         w_in, b_in.reshape(HID // LO, LO), w_out.T, row(b_out), row(layer_scale),
     )
     out_a, grad_states, grad_kernel, grad_win, grad_wout = pl.pallas_call(
-        move,
+        finish,
         out_shape=outs,
-        in_specs=[anywhere] * 5,
+        in_specs=[anywhere] * 4,
         out_specs=(anywhere,) * 5,
-        scratch_shapes=[pltpu.VMEM(o.shape, o.dtype) for o in outs]
-        + [pltpu.SemaphoreType.DMA((5,)), pltpu.SemaphoreType.DMA((5,))],
-        name="move",
+        scratch_shapes=[pltpu.VMEM(o.shape, o.dtype) for o in outs[:3]]
+        + [buf(2, 16, PIECE, LO, dtype=BF16), buf(CH, HID), buf(CH, HID)]
+        + [pltpu.SemaphoreType.DMA((4,)), pltpu.SemaphoreType.DMA((5,))],
+        compiler_params=pltpu.CompilerParams(vmem_limit_bytes=60 * 1024 * 1024),
+        name="finish",
     )(*found)
     return out_a, grad_states, grad_kernel, grad_win, grad_wout.T
 

time: 71.7 us -> 64.6 us (0.901)
  Pallas kernels: 70.9 us -> 63.8 us
    pallas_call x2, Pallas kernels: 70.9 us -> 63.8 us  [the longest x1 60.9 us: shards(): pl.pallas_call(kernel, out_shape=outs[:3] + (jax.ShapeDtypeStruct((2, 16,...]
where the time goes in v3:
time: 64.6 us; the launch traced here: 64.4 us
  Pallas kernels  63.8 us (99%)
    pallas_call x1, Pallas kernels, shards(): pl.pallas_call(kernel, out_shape=outs[:3] + (jax.ShapeDtypeStruct((2, 16,...  60.9 us
    pallas_call x1, Pallas kernels, shards(): pl.pallas_call(finish, out_shape=outs, in_specs=[anywhere] * 4, out_specs...  2.86 us

profile of v3, /device:TPU:1, one launch (start us, length us, event | category | flops | bytes accessed | tf_op | source)
XLA Modules:
  0.0 64.4 jit_solution(13870583796922763773)
XLA Ops:
  0.6 60.9 %block.1 = (bf16[16,64,192]{2,1,0:T(8,128)(2,1)}, f32[16,64,192]{2,1,0:T(8,128)}, f32[7,7,192]{2,1,0:T(8,128)}, bf16[2,16,80,128]{3,2,1,0:T(8,128)(2,1)}) custom-call(bf16[2,16,64,192]{3,2,1,0:T(8,128)(2,1)} %x_in.1, bf16[16,64,192]{2,1,0:T(8,128)(2,1)} %go_in.1, s32[16,64]{1,0:T(8,128)} %mask_in.1, s32[2048]{0:T(1024)} %partner_in.1, f32[7,7,192]{2,1,0:T(8,128)} %dw_in.1, ...), custom_call_target="tpu_custom_call" | custom-call | tf_op jit(solution)/shard_map/block/pallas_call | solution.py:863
  61.5 2.9 %finish.1 = (bf16[16,64,192]{2,1,0:T(8,128)(2,1)}, f32[16,64,192]{2,1,0:T(8,128)}, f32[7,7,192]{2,1,0:T(8,128)}, f32[192,768]{1,0:T(8,128)}, f32[192,768]{1,0:T(8,128)}) custom-call(bf16[16,64,192]{2,1,0:T(8,128)(2,1)} %get-tuple-element.14.outa_in, f32[16,64,192]{2,1,0:T(8,128)} %get-tuple-element.15.gs_in, f32[7,7,192]{2,1,0:T(8,128)} %get-tuple-element.16.gk_in, ...), custom_call_target="tpu_custom_call" | custom-call | tf_op jit(solution)/shard_map/finish/pallas_call | solution.py:877

commit v4 on v3

--- a/solution.py
+++ b/solution.py
@@ -48,7 +48,7 @@
     wout_in, bout_in, ls_in,
     outa_out, gs_out, gk_ref, ag_out,
     x_ref, go_ref, mask_ref, partner_ref, dw_ref, dwb_ref, g_ref, lb_ref, win_ref, bin_ref,
-    wout_ref, bout_ref, ls_ref, load_sem, outa_ref, gs_ref, store_sem, gkf, kr0, ksum, kr1, kr3, kag,
+    wout_ref, bout_ref, ls_ref, load_sem, wbt, wot, outa_ref, gs_ref, store_sem, gkf, kr0, ksum, kr1, kr3, kag,
     pd, pz, xb, zb, sx, sz, rlx, rlz, rcx, rcz, fb1, fa1, fz1, vb, va, vz, fb2, fya, fyz, fxa, fxz,
     dp, mb, kt, wa, wb, gw, gwo, gka, flat, b0, r0, hb, r1, r3, ag, ssem, rsem,
 ):
@@ -377,6 +377,11 @@
     wb[0:128] = win_ref[0:128]
     wb[128:192] = jnp.zeros((64, HID), BF16)
     wb[192:256] = win_ref[128:192]
+    for n in range(3):
+        part = slice(256 * n, 256 * n + 256)
+        wbt[part] = wb[:, part].T
+        both = jnp.concatenate([wout_ref[:, part], jnp.zeros((64, 256), BF16)], axis=0)
+        wot[part] = both.T[:, 0:CH]
     eye = jnp.where(
         lax.broadcasted_iota(jnp.int32, (COLS, COLS), 0) == lax.broadcasted_iota(jnp.int32, (COLS, COLS), 1),
         1.0, 0.0,
@@ -444,7 +449,7 @@
             u = dot(low, wa[:, cut]) + bias(s)
             t = jnp.tanh(u * (root_factor + (root_factor * cubic_coef) * (u * u)))
             act = (u * (0.5 + 0.5 * t)).astype(BF16)
-            mixed = mixed + dot(act, wout_ref[:, cut], ((1,), (1,)))
+            mixed = mixed + dot(act, wot[cut])
         mixed = mixed * ls_ref[...]
         here = pl.ds(pl.multiple_of(c * CHUNK, CHUNK), CHUNK)
         m = mb[here]
@@ -460,6 +465,8 @@
         mm = jnp.concatenate([m, m[:, :64]], axis=1)
         go = jnp.concatenate([go_ref[4 * c + r] for r in range(4)], axis=0).astype(F32)
         gl = (mm * (ls_ref[...] * go)).astype(BF16)
+        low_t = low.T
+        gl_t = jnp.concatenate([gl, jnp.zeros((CHUNK, 64), BF16)], axis=1).T[0:CH]
         gn = jnp.zeros((CHUNK, 256), F32)
         for s in range(3):
             cut = slice(256 * s, 256 * s + 256)
@@ -470,10 +477,10 @@
             value = u * half
             slope = half + value * (1.0 - t) * (root_factor + (3.0 * root_factor * cubic_coef) * u2)
             act = value.astype(BF16)
-            gwo[:, cut] += dot(gl, act, ((0,), (0,)))
+            gwo[:, cut] += dot(gl_t, act)
             gh = (dot(gl, wout_ref[:, cut]) * slope).astype(BF16)
-            gw[:, cut] += dot(low, gh, ((0,), (0,)))
-            gn = gn + dot(gh, wb[:, cut], ((1,), (1,)))
+            gw[:, cut] += dot(low_t, gh)
+            gn = gn + dot(gh, wbt[cut])
         nl, nh = gn[:, :LO] * glo, gn[:, LO:] * ghi
         one = jnp.sum(nl + nh, axis=1, keepdims=True) * (1.0 / CH)
         two = jnp.sum(nl * nlo + nh * nhi, axis=1, keepdims=True) * (1.0 / CH)
@@ -521,15 +528,17 @@
     @pl.when(top)
     def _():
         middle_fold(FOLD_B, xb, in_b, fb1, vb, fb2)
-        start_fold(FOLD_A, xb, in_a, fa1)
 
     finish_halo(0, pd, 3, xb, sx, rlx, rcx)
 
     def first_pass(c, carry):
+        @pl.when(top & (c == 2))
+        def _():
+            start_fold(FOLD_A, xb, in_a, fa1)
+
         @pl.when(top & (c == 3))
         def _():
             finish_fold(FOLD_B, pd, 1, vb, fb2)
-            fold_to_y(FOLD_A, xb, in_a, fa1, va, fya)
 
         def both(plane, carry):
             sweep_states(plane, c)
@@ -620,7 +629,7 @@
 
         @pl.when(top & (c == 2))
         def _():
-            fold_to_x(FOLD_A, va, fya, fxa)
+            fold_to_y(FOLD_A, xb, in_a, fa1, va, fya)
 
         kernel_chunk(c)
         return carry
@@ -663,6 +672,10 @@
     ]
 
     def third_pass(c, carry):
+        @pl.when(top & (c == 1))
+        def _():
+            fold_to_x(FOLD_A, va, fya, fxa)
+
         @pl.when(c == 1)
         def _():
             for m in range(1, 16):
@@ -830,6 +843,7 @@
         buf(ROWS, COLS, dtype=jnp.int32), pltpu.SMEM((NLON,), jnp.int32), buf(7, 7, CH),
         buf(1, CH), buf(1, CH), buf(1, CH), buf(CH, HID, dtype=BF16), buf(HID // LO, LO),
         buf(CH, HID, dtype=BF16), buf(1, CH), buf(1, CH), pltpu.SemaphoreType.DMA((13,)),
+        buf(HID, 256, dtype=BF16), buf(HID, CH, dtype=BF16),
         buf(ROWS, COLS, CH, dtype=BF16), buf(ROWS, COLS, CH), pltpu.SemaphoreType.DMA((4,)),
         buf(128, LO), buf(128, LO), buf(16, 8, LO), buf(15, 8, LO), buf(4, 8, LO), buf(16, 8, LO),
     ]

time: 64.6 us -> 63.6 us (0.985)
  Pallas kernels: 63.8 us -> 62.8 us
    pallas_call x1, Pallas kernels: 60.9 us -> 59.9 us  [shards(): pl.pallas_call(kernel, out_shape=outs[:3] + (jax.ShapeDtypeStruct((2, 16,...]
where the time goes in v4:
time: 63.6 us; the launch traced here: 63.4 us
  Pallas kernels  62.8 us (99%)
  between operations  0.64 us (1%)
    pallas_call x1, Pallas kernels, shards(): pl.pallas_call(kernel, out_shape=outs[:3] + (jax.ShapeDtypeStruct((2, 16,...  59.9 us
    pallas_call x1, Pallas kernels, shards(): pl.pallas_call(finish, out_shape=outs, in_specs=[anywhere] * 4, out_specs...  2.86 us

profile of v4, /device:TPU:1, one launch (start us, length us, event | category | flops | bytes accessed | tf_op | source)
XLA Modules:
  0.0 63.4 jit_solution(12610154543925683515)
XLA Ops:
  0.6 59.9 %block.1 = (bf16[16,64,192]{2,1,0:T(8,128)(2,1)}, f32[16,64,192]{2,1,0:T(8,128)}, f32[7,7,192]{2,1,0:T(8,128)}, bf16[2,16,80,128]{3,2,1,0:T(8,128)(2,1)}) custom-call(bf16[2,16,64,192]{3,2,1,0:T(8,128)(2,1)} %x_in.1, bf16[16,64,192]{2,1,0:T(8,128)(2,1)} %go_in.1, s32[16,64]{1,0:T(8,128)} %mask_in.1, s32[2048]{0:T(1024)} %partner_in.1, f32[7,7,192]{2,1,0:T(8,128)} %dw_in.1, ...), custom_call_target="tpu_custom_call" | custom-call | tf_op jit(solution)/shard_map/block/pallas_call | solution.py:877
  60.6 2.9 %finish.1 = (bf16[16,64,192]{2,1,0:T(8,128)(2,1)}, f32[16,64,192]{2,1,0:T(8,128)}, f32[7,7,192]{2,1,0:T(8,128)}, f32[192,768]{1,0:T(8,128)}, f32[192,768]{1,0:T(8,128)}) custom-call(bf16[16,64,192]{2,1,0:T(8,128)(2,1)} %get-tuple-element.14.outa_in, f32[16,64,192]{2,1,0:T(8,128)} %get-tuple-element.15.gs_in, f32[7,7,192]{2,1,0:T(8,128)} %get-tuple-element.16.gk_in, ...), custom_call_target="tpu_custom_call" | custom-call | tf_op jit(solution)/shard_map/finish/pallas_call | solution.py:891
